TPU v7x, 512 devices: a whole 4x4x16 slice. The times are simulated.
512 devices in a mesh: dp: 4 (over y), group: 16 (over x, z_hi), tensor: 8 (over z_lo, core).
Axes of the slice: x: 4, y: 4, z: 16 (z_hi: 4, z_lo: 4; z = z_hi * 4 + z_lo), core: 2. Of those that a mesh axis runs over, the one named last changes fastest.
Arguments:
- queries: bfloat16 [64, 128, 8192], P(('dp', 'group'), None, 'tensor'), parts along dimension 0, may hold values from -9 to 9
- comp_keys: bfloat16 [64, 128, 1024], P(('dp', 'group'), None, 'tensor'), parts along dimension 0, may hold values from -4 to 4
- comp_values: bfloat16 [64, 128, 1024], P(('dp', 'group'), None, 'tensor'), parts along dimension 0, may hold values from -6 to 6
- prompt_keys: bfloat16 [8192, 1024], P(('dp', 'group'), 'tensor'), parts along dimension 0, may hold values from -9 to 9
- prompt_values: bfloat16 [8192, 1024], P(('dp', 'group'), 'tensor'), parts along dimension 0, may hold values from -6 to 6
- out_grad: bfloat16 [64, 128, 8192], P(('dp', 'group'), None, 'tensor'), parts along dimension 0, may hold values from -192 to 192
- lengths: int32 [64], P(('dp', 'group')), parts along dimension 0, may hold values from 1 to 128
- loss_mask: int32 [64, 128], P(('dp', 'group')), parts along dimension 0, may hold values 0 or 1
- buckets: int32 [64], P(('dp', 'group')), parts along dimension 0, may hold values from 0 to 10
Outputs:
- query_grad: float32 [64, 128, 8192], P(('dp', 'group'), None, 'tensor'), parts along dimension 0
- comp_key_grad: float32 [64, 128, 1024], P(('dp', 'group'), None, 'tensor'), parts along dimension 0
- comp_value_grad: float32 [64, 128, 1024], P(('dp', 'group'), None, 'tensor'), parts along dimension 0
- prompt_key_grad: float32 [8192, 1024], P(('dp', 'group'), 'tensor'), parts along dimension 0
- prompt_value_grad: float32 [8192, 1024], P(('dp', 'group'), 'tensor'), parts along dimension 0
There are 4 independent parts, one for each index of `dp`. A program takes and returns all parts, laid end to end along the dimension named above; each array names one. Nothing has to cross between parts.
All inputs are finite; a program needn't handle non-finite values. No bound on the sum of `loss_mask` on one device may be relied on, other than what follows from the above.
Results may differ from a plain program's by a relative error of at most 0.025.
Values may be sent and summed in bfloat16 or wider, within the bound.
No kernel may reach another device: no remote copies, remote signals or barrier semaphores. Data moves between devices by JAX's collectives and lax.ppermute only.
A program may use at most 64 MiB of HBM per device.

v0:
```python
import jax
import jax.numpy as jnp
from jax import lax
from jax.sharding import PartitionSpec as P

HEADS = 64
KV_HEADS = 8
HEAD_DIM = 128


def split_heads(matrix, kv_heads):
    row_count = matrix.shape[0]
    return matrix.reshape(row_count, kv_heads, HEADS // KV_HEADS, HEAD_DIM).transpose(1, 2, 0, 3)


def head_scores(query_heads, key_block):
    kv_heads = query_heads.shape[0]
    keys_split = key_block.reshape(key_block.shape[0], kv_heads, HEAD_DIM)
    return jnp.einsum(
        "grtd,ngd->grtn", query_heads, keys_split, preferred_element_type=jnp.float32
    ) * HEAD_DIM ** (-0.5)


def merge_scores(carried, scores):
    running, partial_sum = carried
    largest = jnp.maximum(running, jnp.max(scores, axis=-1))
    partial_sum = partial_sum * jnp.exp(running - largest) + jnp.sum(
        jnp.exp(scores - largest[..., None]), axis=-1
    )
    return (largest, partial_sum)


def apply_values(prob_half, value_block):
    kv_heads = prob_half.shape[0]
    values_split = value_block.reshape(value_block.shape[0], kv_heads, HEAD_DIM)
    return jnp.einsum("grtn,ngd->grtd", prob_half, values_split, preferred_element_type=jnp.float32)


def score_grads(scores, value_block, grad_heads, log_total, row_delta):
    kv_heads = grad_heads.shape[0]
    values_split = value_block.reshape(value_block.shape[0], kv_heads, HEAD_DIM)
    prob_full = jnp.exp(scores - log_total[..., None])
    prob_half = prob_full.astype(jnp.bfloat16)
    grad_prob = jnp.einsum(
        "grtd,ngd->grtn", grad_heads, values_split, preferred_element_type=jnp.float32
    )
    score_scale = HEAD_DIM ** (-0.5)
    grad_score = (score_scale * prob_full * (grad_prob - row_delta[..., None])).astype(jnp.bfloat16)
    return (prob_half, grad_score)


def query_grad_of(grad_score, key_block):
    kv_heads = grad_score.shape[0]
    keys_split = key_block.reshape(key_block.shape[0], kv_heads, HEAD_DIM)
    return jnp.einsum("grtn,ngd->grtd", grad_score, keys_split, preferred_element_type=jnp.float32)


def key_value_grads(prob_half, grad_score, query_heads, grad_heads):
    key_grad = jnp.einsum(
        "grtn,grtd->ngd", grad_score, query_heads, preferred_element_type=jnp.float32
    )
    value_grad = jnp.einsum(
        "grtn,grtd->ngd", prob_half, grad_heads, preferred_element_type=jnp.float32
    )
    key_count = key_grad.shape[0]
    return jnp.concatenate(
        [key_grad.reshape(key_count, -1), value_grad.reshape(key_count, -1)], axis=1
    )


def body(
    queries,
    comp_keys,
    comp_values,
    prompt_keys,
    prompt_values,
    out_grad,
    lengths,
    loss_mask,
    buckets,
):
    members = lax.axis_size("group")
    comp_len = queries.shape[1]
    kv_width = prompt_keys.shape[1]
    kv_heads = kv_width // HEAD_DIM
    rewards = buckets.astype(jnp.float32)
    length_sum, reward_sum, square_sum = lax.psum(
        (jnp.sum(lengths.astype(jnp.float32)), jnp.sum(rewards), jnp.sum(rewards * rewards)),
        "group",
    )
    reward_mean = reward_sum / members
    variance = square_sum / members - reward_mean * reward_mean
    advantage = (rewards[0] - reward_mean) / jnp.sqrt(variance + 1.0)
    positions = jnp.arange(comp_len, dtype=jnp.int32)
    valid_tokens = (loss_mask[0] * (positions < lengths[0]).astype(jnp.int32)).astype(jnp.float32)
    weights = advantage * valid_tokens * (members * comp_len / length_sum)
    cotangent = (weights[:, None] * out_grad[0].astype(jnp.float32)).astype(jnp.bfloat16)
    query_heads = split_heads(queries[0], kv_heads)
    grad_heads = split_heads(cotangent, kv_heads)
    own_key = comp_keys[0]
    own_value = comp_values[0]
    causal = positions[None, :] <= positions[:, None]
    own_scores = jnp.where(causal, head_scores(query_heads, own_key), -jnp.inf)
    all_keys, all_values = (
        lax.all_gather(prompt_keys, "group", axis=0, tiled=True),
        lax.all_gather(prompt_values, "group", axis=0, tiled=True),
    )
    prompt_len = all_keys.shape[0]
    block_len = min(512, prompt_len)
    key_blocks = all_keys.reshape(prompt_len // block_len, block_len, kv_width)
    value_blocks = all_values.reshape(prompt_len // block_len, block_len, kv_width)

    def max_step(carried, key_block):
        block_scores = head_scores(query_heads, key_block)
        return (merge_scores(carried, block_scores), block_scores)

    stat_shape = own_scores.shape[:3]
    start_state = (jnp.full(stat_shape, -jnp.inf, jnp.float32), jnp.zeros(stat_shape, jnp.float32))
    carried, stored_scores = lax.scan(max_step, start_state, key_blocks)
    running, partial_sum = merge_scores(carried, own_scores)
    log_total = running + jnp.log(partial_sum)

    def out_step(out_accum, blocks):
        block_scores, value_block = blocks
        prob_half = jnp.exp(block_scores - log_total[..., None]).astype(jnp.bfloat16)
        return (out_accum + apply_values(prob_half, value_block), None)

    out_accum, unused = lax.scan(
        out_step, jnp.zeros(query_heads.shape, jnp.float32), (stored_scores, value_blocks)
    )
    own_prob = jnp.exp(own_scores - log_total[..., None]).astype(jnp.bfloat16)
    output = (out_accum + apply_values(own_prob, own_value)).astype(jnp.bfloat16)
    row_delta = jnp.sum(grad_heads.astype(jnp.float32) * output.astype(jnp.float32), axis=-1)
    own_half, own_grad_score = score_grads(own_scores, own_value, grad_heads, log_total, row_delta)
    own_query_grad = query_grad_of(own_grad_score, own_key)
    own_kv = key_value_grads(own_half, own_grad_score, query_heads, grad_heads)
    zero_grad = jnp.zeros(query_heads.shape, jnp.float32)

    def grad_step(query_grad, blocks):
        block_scores, key_block, value_block = blocks
        prob_half, grad_score = score_grads(
            block_scores, value_block, grad_heads, log_total, row_delta
        )
        return (
            query_grad + query_grad_of(grad_score, key_block),
            key_value_grads(prob_half, grad_score, query_heads, grad_heads),
        )

    prompt_query_grad, block_grads = lax.scan(
        grad_step, zero_grad, (stored_scores, key_blocks, value_blocks)
    )
    owned_rows = lax.psum_scatter(
        block_grads.reshape(prompt_len, 2 * kv_width), "group", scatter_dimension=0, tiled=True
    )
    query_grad = (prompt_query_grad + own_query_grad).transpose(2, 0, 1, 3).reshape(comp_len, -1)
    return (
        query_grad[None],
        own_kv[:, :kv_width][None],
        own_kv[:, kv_width:][None],
        owned_rows[:, :kv_width],
        owned_rows[:, kv_width:],
    )


def solution(mesh):
    return jax.shard_map(
        body,
        mesh=mesh,
        in_specs=(
            P(("dp", "group"), None, "tensor"),
            P(("dp", "group"), None, "tensor"),
            P(("dp", "group"), None, "tensor"),
            P(("dp", "group"), "tensor"),
            P(("dp", "group"), "tensor"),
            P(("dp", "group"), None, "tensor"),
            P(("dp", "group")),
            P(("dp", "group"), None),
            P(("dp", "group")),
        ),
        out_specs=(
            P(("dp", "group"), None, "tensor"),
            P(("dp", "group"), None, "tensor"),
            P(("dp", "group"), None, "tensor"),
            P(("dp", "group"), "tensor"),
            P(("dp", "group"), "tensor"),
        ),
        check_vma=False,
    )
```

profile of v0, /device:TPU:1, one launch (start us, length us, event | category | flops | bytes accessed | tf_op | source)
XLA Modules:
  0.0 401.6 jit_solution(15545250686349632354)
XLA Ops:
  8.6 55.1 %all-reduce = (f32[]{:T(128)}, f32[]{:T(128)}, f32[]{:T(128)}) all-reduce(f32[]{:T(128)} %bitcast.15, f32[]{:T(128)} %bitcast.11, f32[]{:T(128)} %bitcast.12), channel_id=1, replica_groups=mesh['dp'=4,'group'=16,'tensor'=8] {'group'}, use_global_device_ids=true, to_apply=%region_8.9 | all-reduce | flops 3 | bytes 24 | tf_op jit(solution)/shard_map/psum | solution.py:87
  70.7 47.7 %all_gather.6 = bf16[2048,128]{1,0:T(8,128)(2,1)} all-gather(bf16[128,128]{1,0:T(8,128)(2,1)S(1)} %copy-done.10), channel_id=1, replica_groups=mesh['dp'=4,'group'=16,'tensor'=8] {'group'}, dimensions={0}, use_global_device_ids=true | all-gather | bytes 557056 | tf_op jit(solution)/shard_map/all_gather | solution.py:105
  118.4 27.2 %while.39 = (s32[]{:T(128)}, f32[1,8,128]{2,1,0:T(8,128)S(1)}, f32[1,8,128]{2,1,0:T(8,128)S(1)}, f32[4,1,8,128,512]{4,3,2,1,0:T(8,128)}, bf16[4,512,128]{2,1,0:T...) while((s32[]{:T(128)}, f32[1,8,128]{2,1,0:T(8,128)S(1)}, ...), condition=%wide.region_3.0_spmd.clone, body=%wide.region_0.3_spmd.clone.sunk | while | flops 137368576 | bytes 17224800 | solution.py:119
  118.4 1.3 bitcast_reduce_fusion.2
  120.1 1.5 multiply_bitcast_fusion.2
  121.6 1.9 copy.60
  123.5 1.6 constant_dynamic-update-slice_fusion.4
  126.9 1.5 multiply_bitcast_fusion.2
  128.4 1.9 copy.60
  130.3 1.6 constant_dynamic-update-slice_fusion.4
  131.9 1.3 bitcast_reduce_fusion.2
  133.7 1.5 multiply_bitcast_fusion.2
  135.2 1.9 copy.60
  137.1 1.6 constant_dynamic-update-slice_fusion.4
  138.7 1.3 bitcast_reduce_fusion.2
  140.5 1.5 multiply_bitcast_fusion.2
  142.0 1.9 copy.60
  143.9 1.6 constant_dynamic-update-slice_fusion.4
  145.5 51.8 %all_gather.7 = bf16[2048,128]{1,0:T(8,128)(2,1)} all-gather(bf16[128,128]{1,0:T(8,128)(2,1)S(1)} %copy-done.11), channel_id=1, replica_groups=mesh['dp'=4,'group'=16,'tensor'=8] {'group'}, dimensions={0}, use_global_device_ids=true | all-gather | bytes 557056 | tf_op jit(solution)/shard_map/all_gather | solution.py:106
  198.7 8.8 %while.40 = (s32[]{:T(128)}, f32[1,8,128,128]{3,2,1,0:T(8,128)S(1)}, f32[4,1,8,128,512]{4,3,2,1,0:T(8,128)}, f32[1,8,128]{2,1,0:T(8,128)S(1)}, bf16[4,512,128]{2,1,0:T(8,128)(2,1)}, /*index=5*/s32[]{:T(128)}, s32[]{:T(128)}) while((s32[]{:T(128)}, f32[1,8,128,128]{3,2,1,0:T(8,128)S(1)}, f32[4,1,8,128,512]{4,3,2,1,0:T(8,128)}, ...), condition=%wide.region_10.11_spmd.clone, body=%wide.region_9.10_spmd.clone.sunk | while | flops 135528448 | bytes 3282007 | solution.py:128
  198.7 2.2 fusion.80
  201.0 2.2 fusion.80
  203.1 2.2 fusion.80
  205.3 2.2 fusion.80
  208.0 45.7 %while.41 = (s32[]{:T(128)}, f32[1,8,128,128]{3,2,1,0:T(8,128)}, f32[4,512,256]{2,1,0:T(8,128)}, f32[4,1,8,128,512]{4,3,2,1,0:T(8,128)}, f32[1,8,128]{2,1,0:T(8,...) while((s32[]{:T(128)}, f32[1,8,128,128]{3,2,1,0:T(8,128)}, ...), condition=%wide.region_13.14_spmd.clone, body=%wide.region_12.13_spmd.clone.sunk | while | flops 540934144 | bytes 25704124 | solution.py:149
  208.0 1.9 constant_dynamic-slice_fusion.2
  209.9 1.8 copy.61
  211.7 2.3 fusion.89
  214.0 1.4 convolution_bitcast_fusion.11
  217.1 1.5 fusion.90
  219.5 1.9 constant_dynamic-slice_fusion.2
  221.4 1.8 copy.61
  223.2 2.3 fusion.89
  225.4 1.4 convolution_bitcast_fusion.11
  228.6 1.5 fusion.90
  230.9 1.9 constant_dynamic-slice_fusion.2
  232.8 1.8 copy.61
  234.6 2.3 fusion.89
  236.9 1.4 convolution_bitcast_fusion.11
  240.0 1.5 fusion.90
  242.3 1.9 constant_dynamic-slice_fusion.2
  244.2 1.8 copy.61
  246.0 2.3 fusion.89
  248.3 1.4 convolution_bitcast_fusion.11
  251.4 1.5 fusion.90
  257.5 1.8 convolution_bitcast_fusion.7
  259.3 134.0 %reduce-scatter.2.cloned.1.call-done = f32[128,256]{1,0:T(8,128)} async-done(((f32[2048,256]{1,0:T(8,128)}), f32[128,256]{1,0:T(8,128)}) %reduce-scatter.2.cloned.1.call-update) | async-done | bytes 131088 | tf_op jit(solution)/shard_map/reduce_scatter | solution.py:152
  393.2 1.5 fusion.54
  (96 shorter events, 22.0 us)
Async XLA Ops:
  7.2 190.2 %copy-start = (bf16[1,128,128]{2,1,0:T(8,128)(2,1)S(1)}, bf16[1,128,128]{2,1,0:T(8,128)(2,1)}, u32[]{:S(2)}) copy-start(bf16[1,128,128]{2,1,0:T(8,128)(2,1)} %param.16) | copy-start | bytes 98308
  7.2 61.5 %copy-start.8 = (bf16[1,128,1024]{2,1,0:T(8,128)(2,1)S(1)}, bf16[1,128,1024]{2,1,0:T(8,128)(2,1)}, u32[]{:S(2)}) copy-start(bf16[1,128,1024]{2,1,0:T(8,128)(2,1)} %param.15) | copy-start | bytes 786436
  7.2 63.5 %copy-start.10 = (bf16[128,128]{1,0:T(8,128)(2,1)S(1)}, bf16[128,128]{1,0:T(8,128)(2,1)}, u32[]{:S(2)}) copy-start(bf16[128,128]{1,0:T(8,128)(2,1)} %param.18) | copy-start | bytes 98308
  7.2 386.0 %reduce-scatter.2.cloned.1.call-start = ((), (), s32[]{:S(2)}) async-start(), calls=%async_computation.1 | async-start | bytes 2228224 | tf_op jit(solution)/shard_map/reduce_scatter | solution.py:152
  68.6 139.1 %copy-start.6 = (bf16[128,1,8,128]{0,3,2,1:T(8,128)(2,1)}, bf16[128,1,8,128]{0,3,2,1:T(8,128)(2,1)S(1)}, u32[]{:S(2)}) copy-start(bf16[128,1,8,128]{0,3,2,1:T(8,128)(2,1)S(1)} %multiply_convert_fusion) | copy-start | bytes 786436
  118.4 27.2 %copy-start.11 = (bf16[128,128]{1,0:T(8,128)(2,1)S(1)}, bf16[128,128]{1,0:T(8,128)(2,1)}, u32[]{:S(2)}) copy-start(bf16[128,128]{1,0:T(8,128)(2,1)} %param.19) | copy-start | bytes 98308
  198.6 9.1 %copy-start.4 = (f32[8,128,128]{1,2,0:T(8,128)}, f32[8,128,128]{1,2,0:T(8,128)S(1)}, u32[]{:S(2)}) copy-start(f32[8,128,128]{1,2,0:T(8,128)S(1)} %get-tuple-element.273) | copy-start | bytes 1572868
  198.7 9.0 %copy-start.9 = (bf16[1,128,128]{2,1,0:T(8,128)(2,1)S(1)}, bf16[1,128,128]{2,1,0:T(8,128)(2,1)}, u32[]{:S(2)}) copy-start(bf16[1,128,128]{2,1,0:T(8,128)(2,1)} %param.17) | copy-start | bytes 98308
  216.0 1.2 copy-start.1
  218.7 0.8 copy-start.2
  227.4 1.1 copy-start.1
  230.1 0.8 copy-start.2
  238.9 1.1 copy-start.1
  241.5 0.8 copy-start.2
  250.3 1.1 copy-start.1
  252.9 0.8 copy-start.2
  253.7 1.0 copy-start.3
  253.7 1.2 copy-start.5
  253.7 1.3 copy-start.7
Sparse Core Ops, SparseCore 0:
  253.9 139.3 reduce-scatter.1
where the time goes:
time: 403 us; the launch traced here: 402 us
  blocking collectives  155 us (38%)
  waiting for transfers between devices  134 us (33%)
  local copies, waits for them, and re-layouts  44 us (11%)
  matrix products  41.2 us (10%)
  between operations  18.7 us (5%)
  other arithmetic  8.47 us (2%)
    reduce_scatter x1, waiting for transfers between devices, body(): lax.psum_scatter(block_grads.reshape(prompt_len, 2 * kv_width), 'group',...  134 us
    psum x1, blocking collectives, body(): lax.psum((jnp.sum(lengths.astype(jnp.float32)), jnp.sum(rewards), jnp.sum...  55.1 us
    all_gather x1, blocking collectives, body(): lax.all_gather(prompt_values, 'group', axis=0, tiled=True)  51.8 us
    all_gather x1, blocking collectives, body(): lax.all_gather(prompt_keys, 'group', axis=0, tiled=True)  47.7 us
    dynamic_slice x8, local copies, waits for them, and re-layouts, body(): lax.scan(out_step, jnp.zeros(query_heads.shape, jnp.float32), (stored_sco...  14.7 us
    dynamic_update_slice x8, local copies, waits for them, and re-layouts, body(): carried, stored_scores = lax.scan(max_step, start_state, key_blocks)  14.1 us
    dot_general x5, matrix products, score_grads(): jnp.einsum('grtd,ngd->grtn', grad_heads, values_split, preferred_element_...  9.27 us
    dot_general x5, matrix products, apply_values(): jnp.einsum('grtn,ngd->grtd', prob_half, values_split, preferred_element_t...  8.96 us
  transfers between devices with their start and end apart: 1, of which 1 were waited for; matrix products, arithmetic and copies ran while one was open for 1% of the time, Pallas kernels for 0%

commit v1 on v0

v1 whole, which is shorter than its diff:
```python
import functools

import jax
import jax.numpy as jnp
from jax import lax
from jax.experimental import pallas as pl
from jax.experimental.pallas import tpu as pltpu
from jax.sharding import PartitionSpec as P

HEAD_DIM = 128
SCALE = HEAD_DIM ** (-0.5)
LOG2E = 1.4426950408889634
META = 16
TILE = 256
NT = (((1,), (1,)), ((), ()))


def fold_rows(values, op):
    rows, cols = values.shape
    return op(values.reshape(rows // 8, 8, cols), axis=0)


def attention_kernel(
    members, row_chunk,
    gath, own_key, own_value, queries, grads, mine, mask,
    query_grad, own_key_grad, own_value_grad, prompt_grads,
    keys, values, keys_t, q_rows, g_rows, weight_row, scores, grad_prob, grad_score, key_acc, value_acc, dq_t,
):
    own_len = own_key.shape[0]
    comp_len, width = queries.shape
    heads = width // HEAD_DIM
    block = gath.shape[1] - META
    half = block // 2
    prompt_len = members * half
    total = prompt_len + own_len
    for i in range(members):
        keys[i * half:(i + 1) * half, :] = gath[i, :half, :]
        values[i * half:(i + 1) * half, :] = gath[i, half:block, :]
    keys[prompt_len:, :] = own_key[...]
    values[prompt_len:, :] = own_value[...]
    for i in range(total // 128):
        keys_t[:, i * 128:(i + 1) * 128] = keys[i * 128:(i + 1) * 128, :].T
    for h in range(heads):
        q_rows[h * comp_len:(h + 1) * comp_len, :] = queries[:, h * HEAD_DIM:(h + 1) * HEAD_DIM]
        g_rows[h * comp_len:(h + 1) * comp_len, :] = grads[:, h * HEAD_DIM:(h + 1) * HEAD_DIM]

    length_sum = jnp.zeros((1, 128), jnp.float32)
    reward_sum = jnp.zeros((1, 128), jnp.float32)
    square_sum = jnp.zeros((1, 128), jnp.float32)
    for i in range(members):
        meta = gath[i, block:block + META, :].astype(jnp.float32)
        reward = meta[1:2, :]
        length_sum += meta[0:1, :]
        reward_sum += reward
        square_sum += reward * reward
    own_meta = mine[block:block + META, :].astype(jnp.float32)
    reward_mean = reward_sum / members
    variance = square_sum / members - reward_mean * reward_mean
    advantage = (own_meta[1:2, :] - reward_mean) / jnp.sqrt(variance + 1.0)
    positions = lax.broadcasted_iota(jnp.int32, (1, comp_len), 1).astype(jnp.float32)
    valid = jnp.where(positions < own_meta[0:1, :], mask[...].astype(jnp.float32), 0.0)
    weights = advantage * valid * (members * comp_len / length_sum)
    weight_row[...] = jnp.concatenate([weights] * (TILE // comp_len), axis=1)

    chunks = total // row_chunk

    def tile_step(j, _):
        cols = pl.ds(pl.multiple_of(j * TILE, TILE), TILE)
        q_tile = q_rows[cols, :]
        g_tile = g_rows[cols, :]
        largest = jnp.full((8, TILE), -jnp.inf, jnp.float32)
        for i in range(chunks):
            rows = slice(i * row_chunk, (i + 1) * row_chunk)
            s = lax.dot_general(keys[rows, :], q_tile, NT, preferred_element_type=jnp.float32)
            if (i + 1) * row_chunk > prompt_len:
                own = s[row_chunk - own_len:, :]
                key_pos = lax.broadcasted_iota(jnp.int32, own.shape, 0)
                row_pos = lax.broadcasted_iota(jnp.int32, own.shape, 1) % comp_len
                own = jnp.where(key_pos <= row_pos, own, -jnp.inf)
                s = jnp.concatenate([s[:row_chunk - own_len, :], own], axis=0)
            scores[rows, :] = s
            largest = jnp.maximum(largest, fold_rows(s, jnp.max))
        top = jnp.max(largest, axis=0, keepdims=True)
        sums = jnp.zeros((8, TILE), jnp.float32)
        dots = jnp.zeros((8, TILE), jnp.float32)
        for i in range(chunks):
            rows = slice(i * row_chunk, (i + 1) * row_chunk)
            dp = lax.dot_general(values[rows, :], g_tile, NT, preferred_element_type=jnp.float32)
            e = jnp.exp2((scores[rows, :] - top) * (SCALE * LOG2E))
            scores[rows, :] = e
            grad_prob[rows, :] = dp
            sums += fold_rows(e, jnp.sum)
            dots += fold_rows(e * dp, jnp.sum)
        inverse = 1.0 / jnp.sum(sums, axis=0, keepdims=True)
        delta = jnp.sum(dots, axis=0, keepdims=True) * inverse
        factor = weight_row[...] * inverse
        for i in range(chunks):
            rows = slice(i * row_chunk, (i + 1) * row_chunk)
            p = scores[rows, :] * factor
            ds = (p * ((grad_prob[rows, :] - delta) * SCALE)).astype(jnp.bfloat16)
            grad_score[rows, :] = ds
            dv = jnp.dot(p.astype(jnp.bfloat16), g_tile, preferred_element_type=jnp.float32)
            dk = jnp.dot(ds, q_tile, preferred_element_type=jnp.float32)
            value_acc[rows, :] = jnp.where(j == 0, dv, value_acc[rows, :] + dv)
            key_acc[rows, :] = jnp.where(j == 0, dk, key_acc[rows, :] + dk)
        dq_t[j] = jnp.dot(keys_t[...], grad_score[...], preferred_element_type=jnp.float32)
        return 0

    key_acc[...] = jnp.zeros_like(key_acc)
    value_acc[...] = jnp.zeros_like(value_acc)
    lax.fori_loop(0, width // TILE, tile_step, 0)

    for h in range(heads):
        j, k = divmod(h * HEAD_DIM, TILE)
        query_grad[:, h * HEAD_DIM:(h + 1) * HEAD_DIM] = dq_t[j, :, k:k + HEAD_DIM].T
    for i in range(members):
        prompt_grads[i, :half, :] = key_acc[i * half:(i + 1) * half, :].astype(jnp.bfloat16)
        prompt_grads[i, half:, :] = value_acc[i * half:(i + 1) * half, :].astype(jnp.bfloat16)
    own_key_grad[...] = key_acc[prompt_len:, :]
    own_value_grad[...] = value_acc[prompt_len:, :]


def attention(gath, own_key, own_value, queries, grads, mine, mask):
    members, packed, dim = gath.shape
    block = packed - META
    comp_len, width = queries.shape
    own_len = own_key.shape[0]
    total = members * block // 2 + own_len
    f32, bf16 = jnp.float32, jnp.bfloat16
    vmem = pl.BlockSpec(memory_space=pltpu.VMEM)
    row_chunk = 544
    units = total * comp_len * width
    return pl.pallas_call(
        functools.partial(attention_kernel, members, row_chunk),
        out_shape=(
            jax.ShapeDtypeStruct((comp_len, width), f32),
            jax.ShapeDtypeStruct((own_len, dim), f32),
            jax.ShapeDtypeStruct((own_len, dim), f32),
            jax.ShapeDtypeStruct((members, block, dim), bf16),
        ),
        in_specs=[vmem] * 7,
        out_specs=(vmem,) * 4,
        scratch_shapes=[
            pltpu.VMEM((total, dim), bf16),
            pltpu.VMEM((total, dim), bf16),
            pltpu.VMEM((dim, total), bf16),
            pltpu.VMEM((width, dim), bf16),
            pltpu.VMEM((width, dim), bf16),
            pltpu.VMEM((1, TILE), f32),
            pltpu.VMEM((total, TILE), f32),
            pltpu.VMEM((total, TILE), f32),
            pltpu.VMEM((total, TILE), bf16),
            pltpu.VMEM((total, dim), f32),
            pltpu.VMEM((total, dim), f32),
            pltpu.VMEM((width // TILE, dim, TILE), f32),
        ],
        compiler_params=pltpu.CompilerParams(vmem_limit_bytes=32 * 1024 * 1024),
        cost_estimate=pl.CostEstimate(flops=10 * units, bytes_accessed=4 * units // 100, transcendentals=total * width),
        name="attention",
    )(gath, own_key, own_value, queries, grads, mine, mask)


def body(queries, comp_keys, comp_values, prompt_keys, prompt_values, out_grad, lengths, loss_mask, buckets):
    along_x = lax.axis_size("gx")
    dim = prompt_keys.shape[1]
    row = lax.broadcasted_iota(jnp.int32, (META, dim), 0)
    meta = jnp.where(row == 0, lengths[0], jnp.where(row == 1, buckets[0], 0)).astype(jnp.bfloat16)
    mine = jnp.concatenate([prompt_keys, prompt_values, meta], axis=0)
    column = lax.all_gather(mine, "gz")
    gath = lax.all_to_all(jnp.broadcast_to(column[None], (along_x, *column.shape)), "gx", 0, 0)
    gath = gath.reshape(-1, *mine.shape)
    query_grad, own_key_grad, own_value_grad, prompt_grads = attention(
        gath, comp_keys[0], comp_values[0], queries[0], out_grad[0], mine, loss_mask
    )
    prompt_grads = prompt_grads.reshape(along_x, -1, *prompt_grads.shape[1:])
    terms = lax.all_to_all(prompt_grads, "gx", 0, 0)
    partial = jnp.sum(terms.astype(jnp.float32), axis=0).astype(jnp.bfloat16)
    terms = lax.all_to_all(partial, "gz", 0, 0)
    owned = jnp.sum(terms.astype(jnp.float32), axis=0)
    half = owned.shape[0] // 2
    return (
        query_grad[None],
        own_key_grad[None],
        own_value_grad[None],
        owned[:half],
        owned[half:],
    )


def solution(mesh):
    dp, group, tensor = (mesh.shape[name] for name in ("dp", "group", "tensor"))
    along_z = 4
    split = jax.sharding.Mesh(
        mesh.devices.reshape(dp, group // along_z, along_z, tensor), ("dp", "gx", "gz", "tensor")
    )
    rows = ("dp", "gx", "gz")
    return jax.shard_map(
        body,
        mesh=split,
        in_specs=(
            P(rows, None, "tensor"),
            P(rows, None, "tensor"),
            P(rows, None, "tensor"),
            P(rows, "tensor"),
            P(rows, "tensor"),
            P(rows, None, "tensor"),
            P(rows),
            P(rows, None),
            P(rows),
        ),
        out_specs=(
            P(rows, None, "tensor"),
            P(rows, None, "tensor"),
            P(rows, None, "tensor"),
            P(rows, "tensor"),
            P(rows, "tensor"),
        ),
        check_vma=False,
    )
```

time: 403 us -> 97.3 us (0.24)
  the two profiles are of different devices: /device:TPU:1 before, /device:TPU:56 now
where the time goes in v1:
time: 97.3 us; the launch traced here: 97 us
  blocking collectives  81.3 us (84%)
  Pallas kernels  11.7 us (12%)
  between operations  2.01 us (2%)
  other arithmetic  1.13 us (1%)
    all_gather x1, blocking collectives, body(): column = lax.all_gather(mine, 'gz')  26.1 us
    all_to_all x1, blocking collectives, body(): terms = lax.all_to_all(partial, 'gz', 0, 0)  23.3 us
    all_to_all x1, blocking collectives, body(): lax.all_to_all(jnp.broadcast_to(column[None], (along_x, *column.shape)),...  17.6 us
    all_to_all x1, blocking collectives, body(): terms = lax.all_to_all(prompt_grads, 'gx', 0, 0)  14.2 us
    pallas_call x1, Pallas kernels, attention(): pl.pallas_call(functools.partial(attention_kernel, members, row_chunk), o...  11.7 us

profile of v1, /device:TPU:56, one launch (start us, length us, event | category | flops | bytes accessed | tf_op | source)
XLA Modules:
  0.0 97.0 jit_solution(10367791774379337956)
XLA Ops:
  1.9 0.1 select_convert_fusion
  2.0 0.8 pad_maximum_fusion.mine
  2.8 26.1 %all-gather = bf16[1088,128]{1,0:T(8,128)(2,1)S(1)} all-gather(bf16[272,128]{1,0:T(8,128)(2,1)S(1)} %pad_maximum_fusion.mine), channel_id=2, replica_groups=mesh['dp'=4,'gx'=4,'gz'=4,'tensor'=8] {'gz'}, dimensions={0}, use_global_device_ids=true | all-gather | bytes 348160 | tf_op jit(solution)/shard_map/all_gather | solution.py:169
  28.9 0.1 broadcast_in_dim.27
  29.1 0.0 copy-start
  29.1 0.0 copy-start.1
  29.1 0.0 copy-start.2
  29.1 0.0 copy-start.3
  29.1 0.0 copy-start.4
  29.1 17.6 %all_to_all.15 = bf16[4,4,272,128]{3,2,1,0:T(8,128)(2,1)S(1)} all-to-all(bf16[4,4,272,128]{3,2,1,0:T(8,128)(2,1)S(1)} %broadcast_in_dim.27), channel_id=1, replica_groups=mesh['dp'=4,'gx'=4,'gz'=4,'tensor'=8] {'gx'}, dimensions={0} | all-to-all | bytes 2228224 | tf_op jit(solution)/shard_map/all_to_all | solution.py:170
  46.8 0.0 copy-done
  46.8 0.0 copy-done.1
  46.8 0.0 copy-done.2
  46.8 0.0 copy-done.3
  46.8 0.0 copy-done.4
  46.8 11.7 %attention.1 = (f32[128,1024]{1,0:T(8,128)}, f32[128,128]{1,0:T(8,128)}, f32[128,128]{1,0:T(8,128)}, bf16[16,256,128]{2,1,0:T(8,128)(2,1)S(1)}) custom-call(bf16[16,272,128]{2,1,0:T(8,128)(2,1)S(1)} %bitcast.14, bf16[128,128]{1,0:T(8,128)(2,1)S(1)} %bitcast.18, bf16[128,128]{1,0:T(8,128)(2,1)S(1)} %bitcast.19, bf16[128,1024]{1,0:T(8,128)(2,1)S(1)} %bitcast.16, ...), custom_call_target="tpu_custom_call" | custom-call | flops 2852126720 | bytes 11408506 | tf_op jit(solution)/shard_map/attention/pallas_call | solution.py:133
  58.5 14.2 %all_to_all.16 = bf16[4,4,256,128]{3,2,1,0:T(8,128)(2,1)S(1)} all-to-all(bf16[4,4,256,128]{3,2,1,0:T(8,128)(2,1)S(1)} %bitcast.15), channel_id=1, replica_groups=mesh['dp'=4,'gx'=4,'gz'=4,'tensor'=8] {'gx'}, dimensions={0} | all-to-all | bytes 2097152 | tf_op jit(solution)/shard_map/all_to_all | solution.py:176
  72.7 0.2 reduce_sum.21
  72.9 23.3 %all_to_all.17 = bf16[4,256,128]{2,1,0:T(8,128)(2,1)S(1)} all-to-all(bf16[4,256,128]{2,1,0:T(8,128)(2,1)S(1)} %reduce_sum.21), channel_id=1, replica_groups=mesh['dp'=4,'gx'=4,'gz'=4,'tensor'=8] {'gz'}, dimensions={0} | all-to-all | bytes 524288 | tf_op jit(solution)/shard_map/all_to_all | solution.py:178
  96.3 0.7 fusion
  (3 shorter events, 0.0 us)
Async XLA Ops:
  29.1 17.7 %copy-start = (bf16[1,128,1024]{2,1,0:T(8,128)(2,1)S(1)}, bf16[1,128,1024]{2,1,0:T(8,128)(2,1)}, u32[]{:S(2)}) copy-start(bf16[1,128,1024]{2,1,0:T(8,128)(2,1)} %param.9) | copy-start | bytes 786436
  29.1 17.7 %copy-start.1 = (bf16[1,128,1024]{2,1,0:T(8,128)(2,1)S(1)}, bf16[1,128,1024]{2,1,0:T(8,128)(2,1)}, u32[]{:S(2)}) copy-start(bf16[1,128,1024]{2,1,0:T(8,128)(2,1)} %param.14) | copy-start | bytes 786436
  29.1 17.7 %copy-start.2 = (bf16[1,128,128]{2,1,0:T(8,128)(2,1)S(1)}, bf16[1,128,128]{2,1,0:T(8,128)(2,1)}, u32[]{:S(2)}) copy-start(bf16[1,128,128]{2,1,0:T(8,128)(2,1)} %param.10) | copy-start | bytes 98308
  29.1 17.7 %copy-start.3 = (bf16[1,128,128]{2,1,0:T(8,128)(2,1)S(1)}, bf16[1,128,128]{2,1,0:T(8,128)(2,1)}, u32[]{:S(2)}) copy-start(bf16[1,128,128]{2,1,0:T(8,128)(2,1)} %param.11) | copy-start | bytes 98308
  29.1 17.7 %copy-start.4 = (s32[1,128]{1,0:T(1,128)S(1)}, s32[1,128]{1,0:T(1,128)}, u32[]{:S(2)}) copy-start(s32[1,128]{1,0:T(1,128)} %mask.1) | copy-start | bytes 1540

commit v2 on v1

--- a/solution.py
+++ b/solution.py
@@ -11,7 +11,8 @@
 SCALE = HEAD_DIM ** (-0.5)
 LOG2E = 1.4426950408889634
 META = 16
-TILE = 256
+Z_ORDER = [2, 1, 0, 3]
+TILE = 512
 NT = (((1,), (1,)), ((), ()))
 
 
@@ -24,7 +25,7 @@
     members, row_chunk,
     gath, own_key, own_value, queries, grads, mine, mask,
     query_grad, own_key_grad, own_value_grad, prompt_grads,
-    keys, values, keys_t, q_rows, g_rows, weight_row, scores, grad_prob, grad_score, key_acc, value_acc, dq_t,
+    keys, values, keys_t, q_rows, g_rows, weight_row, scores, grad_prob, expo, grad_score, key_acc, value_acc, dq_t,
 ):
     own_len = own_key.shape[0]
     comp_len, width = queries.shape
@@ -64,8 +65,8 @@
 
     chunks = total // row_chunk
 
-    def tile_step(j, _):
-        cols = pl.ds(pl.multiple_of(j * TILE, TILE), TILE)
+    def tile_step(j):
+        cols = slice(j * TILE, (j + 1) * TILE)
         q_tile = q_rows[cols, :]
         g_tile = g_rows[cols, :]
         largest = jnp.full((8, TILE), -jnp.inf, jnp.float32)
@@ -87,28 +88,32 @@
             rows = slice(i * row_chunk, (i + 1) * row_chunk)
             dp = lax.dot_general(values[rows, :], g_tile, NT, preferred_element_type=jnp.float32)
             e = jnp.exp2((scores[rows, :] - top) * (SCALE * LOG2E))
-            scores[rows, :] = e
+            expo[rows, :] = e.astype(jnp.bfloat16)
             grad_prob[rows, :] = dp
             sums += fold_rows(e, jnp.sum)
             dots += fold_rows(e * dp, jnp.sum)
         inverse = 1.0 / jnp.sum(sums, axis=0, keepdims=True)
         delta = jnp.sum(dots, axis=0, keepdims=True) * inverse
         factor = weight_row[...] * inverse
+        column = jnp.concatenate(
+            [jnp.broadcast_to(factor[:, k:k + 128], (128, 128)).T for k in range(0, TILE, 128)], axis=0
+        )
+        g_scaled = (g_tile.astype(jnp.float32) * column).astype(jnp.bfloat16)
+        q_scaled = (q_tile.astype(jnp.float32) * (column * SCALE)).astype(jnp.bfloat16)
         for i in range(chunks):
             rows = slice(i * row_chunk, (i + 1) * row_chunk)
-            p = scores[rows, :] * factor
-            ds = (p * ((grad_prob[rows, :] - delta) * SCALE)).astype(jnp.bfloat16)
+            e = expo[rows, :]
+            ds = (e.astype(jnp.float32) * (grad_prob[rows, :] - delta)).astype(jnp.bfloat16)
             grad_score[rows, :] = ds
-            dv = jnp.dot(p.astype(jnp.bfloat16), g_tile, preferred_element_type=jnp.float32)
-            dk = jnp.dot(ds, q_tile, preferred_element_type=jnp.float32)
-            value_acc[rows, :] = jnp.where(j == 0, dv, value_acc[rows, :] + dv)
-            key_acc[rows, :] = jnp.where(j == 0, dk, key_acc[rows, :] + dk)
-        dq_t[j] = jnp.dot(keys_t[...], grad_score[...], preferred_element_type=jnp.float32)
-        return 0
-
-    key_acc[...] = jnp.zeros_like(key_acc)
-    value_acc[...] = jnp.zeros_like(value_acc)
-    lax.fori_loop(0, width // TILE, tile_step, 0)
+            dv = jnp.dot(e, g_scaled, preferred_element_type=jnp.float32)
+            dk = jnp.dot(ds, q_scaled, preferred_element_type=jnp.float32)
+            value_acc[rows, :] = dv if j == 0 else value_acc[rows, :] + dv
+            key_acc[rows, :] = dk if j == 0 else key_acc[rows, :] + dk
+        dq = jnp.dot(keys_t[...], grad_score[...], preferred_element_type=jnp.float32)
+        dq_t[j] = dq * (factor * SCALE)
+
+    for j in range(width // TILE):
+        tile_step(j)
 
     for h in range(heads):
         j, k = divmod(h * HEAD_DIM, TILE)
@@ -150,6 +155,7 @@
             pltpu.VMEM((total, TILE), f32),
             pltpu.VMEM((total, TILE), f32),
             pltpu.VMEM((total, TILE), bf16),
+            pltpu.VMEM((total, TILE), bf16),
             pltpu.VMEM((total, dim), f32),
             pltpu.VMEM((total, dim), f32),
             pltpu.VMEM((width // TILE, dim, TILE), f32),
@@ -162,8 +168,7 @@
 
 def body(queries, comp_keys, comp_values, prompt_keys, prompt_values, out_grad, lengths, loss_mask, buckets):
     along_x = lax.axis_size("gx")
-    dim = prompt_keys.shape[1]
-    row = lax.broadcasted_iota(jnp.int32, (META, dim), 0)
+    row = lax.broadcasted_iota(jnp.int32, (META, prompt_keys.shape[1]), 0)
     meta = jnp.where(row == 0, lengths[0], jnp.where(row == 1, buckets[0], 0)).astype(jnp.bfloat16)
     mine = jnp.concatenate([prompt_keys, prompt_values, meta], axis=0)
     column = lax.all_gather(mine, "gz")
@@ -175,7 +180,7 @@
     prompt_grads = prompt_grads.reshape(along_x, -1, *prompt_grads.shape[1:])
     terms = lax.all_to_all(prompt_grads, "gx", 0, 0)
     partial = jnp.sum(terms.astype(jnp.float32), axis=0).astype(jnp.bfloat16)
-    terms = lax.all_to_all(partial, "gz", 0, 0)
+    terms = lax.all_to_all(jnp.stack([partial[i] for i in Z_ORDER]), "gz", 0, 0, axis_index_groups=[Z_ORDER])
     owned = jnp.sum(terms.astype(jnp.float32), axis=0)
     half = owned.shape[0] // 2
     return (

time: 97.3 us -> 90 us (0.925)
  blocking collectives: 81.3 us -> 76.8 us
  Pallas kernels: 11.7 us -> 8.9 us
    all_to_all x1, blocking collectives: 23.3 us -> 18.8 us  [body(): lax.all_to_all(jnp.stack([partial[i] for i in Z_ORDER]), 'gz', 0, 0, axis...]
    pallas_call x1, Pallas kernels: 11.7 us -> 8.9 us  [attention(): pl.pallas_call(functools.partial(attention_kernel, members, row_chunk), o...]
where the time goes in v2:
time: 90 us; the launch traced here: 89.7 us
  blocking collectives  76.8 us (85%)
  Pallas kernels  8.9 us (10%)
  between operations  2.02 us (2%)
  other arithmetic  1.16 us (1%)
    all_gather x1, blocking collectives, body(): column = lax.all_gather(mine, 'gz')  26.1 us
    all_to_all x1, blocking collectives, body(): lax.all_to_all(jnp.stack([partial[i] for i in Z_ORDER]), 'gz', 0, 0, axis...  18.8 us
    all_to_all x1, blocking collectives, body(): lax.all_to_all(jnp.broadcast_to(column[None], (along_x, *column.shape)),...  17.6 us
    all_to_all x1, blocking collectives, body(): terms = lax.all_to_all(prompt_grads, 'gx', 0, 0)  14.2 us
    pallas_call x1, Pallas kernels, attention(): pl.pallas_call(functools.partial(attention_kernel, members, row_chunk), o...  8.9 us

profile of v2, /device:TPU:56, one launch (start us, length us, event | category | flops | bytes accessed | tf_op | source)
XLA Modules:
  0.0 89.7 jit_solution(10006247111281914367)
XLA Ops:
  1.9 0.1 select_convert_fusion
  2.0 0.8 pad_maximum_fusion.1.mine
  2.8 26.1 %all-gather = bf16[1088,128]{1,0:T(8,128)(2,1)S(1)} all-gather(bf16[272,128]{1,0:T(8,128)(2,1)S(1)} %pad_maximum_fusion.1.mine), channel_id=2, replica_groups=mesh['dp'=4,'gx'=4,'gz'=4,'tensor'=8] {'gz'}, dimensions={0}, use_global_device_ids=true | all-gather | bytes 348160 | tf_op jit(solution)/shard_map/all_gather | solution.py:174
  28.9 0.1 broadcast_in_dim.27
  29.1 0.0 copy-start
  29.1 0.0 copy-start.1
  29.1 0.0 copy-start.2
  29.1 0.0 copy-start.3
  29.1 0.0 copy-start.4
  29.1 17.6 %all_to_all.15 = bf16[4,4,272,128]{3,2,1,0:T(8,128)(2,1)S(1)} all-to-all(bf16[4,4,272,128]{3,2,1,0:T(8,128)(2,1)S(1)} %broadcast_in_dim.27), channel_id=1, replica_groups=mesh['dp'=4,'gx'=4,'gz'=4,'tensor'=8] {'gx'}, dimensions={0} | all-to-all | bytes 2228224 | tf_op jit(solution)/shard_map/all_to_all | solution.py:175
  46.8 0.0 copy-done
  46.8 0.0 copy-done.1
  46.8 0.0 copy-done.2
  46.8 0.0 copy-done.3
  46.8 0.0 copy-done.4
  46.8 8.9 %attention.1 = (f32[128,1024]{1,0:T(8,128)}, f32[128,128]{1,0:T(8,128)}, f32[128,128]{1,0:T(8,128)}, bf16[16,256,128]{2,1,0:T(8,128)(2,1)S(1)}) custom-call(bf16[16,272,128]{2,1,0:T(8,128)(2,1)S(1)} %bitcast.14, bf16[128,128]{1,0:T(8,128)(2,1)S(1)} %bitcast.18, bf16[128,128]{1,0:T(8,128)(2,1)S(1)} %bitcast.19, bf16[128,1024]{1,0:T(8,128)(2,1)S(1)} %bitcast.16, ...), custom_call_target="tpu_custom_call" | custom-call | flops 2852126720 | bytes 11408506 | tf_op jit(solution)/shard_map/attention/pallas_call | solution.py:138
  55.7 14.2 %all_to_all.16 = bf16[4,4,256,128]{3,2,1,0:T(8,128)(2,1)S(1)} all-to-all(bf16[4,4,256,128]{3,2,1,0:T(8,128)(2,1)S(1)} %bitcast.15), channel_id=1, replica_groups=mesh['dp'=4,'gx'=4,'gz'=4,'tensor'=8] {'gx'}, dimensions={0} | all-to-all | bytes 2097152 | tf_op jit(solution)/shard_map/all_to_all | solution.py:181
  69.9 0.2 reduce_sum.21
  70.2 18.8 %all_to_all.17 = bf16[4,256,128]{2,1,0:T(8,128)(2,1)S(1)} all-to-all(bf16[4,256,128]{2,1,0:T(8,128)(2,1)S(1)} %pad_maximum_fusion), channel_id=1, replica_groups={{16,8,0,24},{17,9,1,25},{18,10,2,26},{19,11,3,27},{20,12,4,28},{21,13,5..., dimensions={0} | all-to-all | bytes 524288 | tf_op jit(solution)/shard_map/all_to_all | solution.py:183
  89.0 0.7 fusion.1
  (5 shorter events, 0.1 us)
Async XLA Ops:
  29.1 17.7 %copy-start = (bf16[1,128,1024]{2,1,0:T(8,128)(2,1)S(1)}, bf16[1,128,1024]{2,1,0:T(8,128)(2,1)}, u32[]{:S(2)}) copy-start(bf16[1,128,1024]{2,1,0:T(8,128)(2,1)} %param.9) | copy-start | bytes 786436
  29.1 17.7 %copy-start.1 = (bf16[1,128,1024]{2,1,0:T(8,128)(2,1)S(1)}, bf16[1,128,1024]{2,1,0:T(8,128)(2,1)}, u32[]{:S(2)}) copy-start(bf16[1,128,1024]{2,1,0:T(8,128)(2,1)} %param.14) | copy-start | bytes 786436
  29.1 17.7 %copy-start.2 = (bf16[1,128,128]{2,1,0:T(8,128)(2,1)S(1)}, bf16[1,128,128]{2,1,0:T(8,128)(2,1)}, u32[]{:S(2)}) copy-start(bf16[1,128,128]{2,1,0:T(8,128)(2,1)} %param.10) | copy-start | bytes 98308
  29.1 17.7 %copy-start.3 = (bf16[1,128,128]{2,1,0:T(8,128)(2,1)S(1)}, bf16[1,128,128]{2,1,0:T(8,128)(2,1)}, u32[]{:S(2)}) copy-start(bf16[1,128,128]{2,1,0:T(8,128)(2,1)} %param.11) | copy-start | bytes 98308
  29.1 17.7 %copy-start.4 = (s32[1,128]{1,0:T(1,128)S(1)}, s32[1,128]{1,0:T(1,128)}, u32[]{:S(2)}) copy-start(s32[1,128]{1,0:T(1,128)} %mask.1) | copy-start | bytes 1540

commit v3 on v2

v3 whole, which is shorter than its diff:
```python
import jax
import jax.numpy as jnp
from jax import lax
from jax.experimental import pallas as pl
from jax.experimental.pallas import tpu as pltpu
from jax.sharding import PartitionSpec as P

HEAD_DIM = 128
SCALE = HEAD_DIM ** (-0.5)
LOG2E = 1.4426950408889634
META = 16
Z_ORDER = [2, 1, 0, 3]
SHIFTS = (0, 1, 3, 2)
TILE = 512
NT = (((1,), (1,)), ((), ()))


def fold_rows(values, op):
    rows, cols = values.shape
    return op(values.reshape(rows // 8, 8, cols), axis=0)


def copy_column(column, key_rows, value_rows, start):
    blocks, packed, _ = column.shape
    half = (packed - META) // 2
    for i in range(blocks):
        rows = slice(start + i * half, start + (i + 1) * half)
        key_rows[rows, :] = column[i, :half, :]
        value_rows[rows, :] = column[i, half:2 * half, :]


def transpose_rows(rows_ref, out):
    for i in range(0, rows_ref.shape[0], 128):
        out[:, i:i + 128] = rows_ref[i:i + 128, :].T


def forward_tile(cols, key_rows, value_rows, q_tile, g_tile, scores, expo, grad_prob, stats, own_len, comp_len):
    total = key_rows.shape[0]
    width = q_tile.shape[0]
    chunk = 512 if total % 512 == 0 else total // 2
    largest = jnp.full((8, width), -jnp.inf, jnp.float32)
    for i in range(0, total, chunk):
        rows = slice(i, i + chunk)
        s = lax.dot_general(key_rows[rows, :], q_tile, NT, preferred_element_type=jnp.float32)
        if own_len and i + chunk == total:
            own = s[chunk - own_len:, :]
            key_pos = lax.broadcasted_iota(jnp.int32, own.shape, 0)
            row_pos = lax.broadcasted_iota(jnp.int32, own.shape, 1) % comp_len
            own = jnp.where(key_pos <= row_pos, own, -jnp.inf)
            s = jnp.concatenate([s[:chunk - own_len, :], own], axis=0)
        scores[rows, :] = s
        largest = jnp.maximum(largest, fold_rows(s, jnp.max))
    top = jnp.max(largest, axis=0, keepdims=True)
    sums = jnp.zeros((8, width), jnp.float32)
    dots = jnp.zeros((8, width), jnp.float32)
    for i in range(0, total, chunk):
        rows = slice(i, i + chunk)
        dp = lax.dot_general(value_rows[rows, :], g_tile, NT, preferred_element_type=jnp.float32)
        e = jnp.exp2((scores[rows, :] - top) * (SCALE * LOG2E))
        expo[rows, cols] = e.astype(jnp.bfloat16)
        grad_prob[rows, cols] = dp
        sums += fold_rows(e, jnp.sum)
        dots += fold_rows(e * dp, jnp.sum)
    stats[0:8, cols] = jnp.broadcast_to(top, (8, width))
    stats[8:16, cols] = sums
    stats[16:24, cols] = dots


def tiles_of(width):
    return [slice(j, j + TILE) for j in range(0, width, TILE)]


def own_kernel(
    column, own_key, own_value, queries, grads,
    q_rows, g_rows, keys_t, expo, grad_prob, stats,
    key_rows, value_rows, scores,
):
    comp_len, width = queries.shape
    own_len = own_key.shape[0]
    for h in range(width // HEAD_DIM):
        q_rows[h * comp_len:(h + 1) * comp_len, :] = queries[:, h * HEAD_DIM:(h + 1) * HEAD_DIM]
        g_rows[h * comp_len:(h + 1) * comp_len, :] = grads[:, h * HEAD_DIM:(h + 1) * HEAD_DIM]
    copy_column(column, key_rows, value_rows, 0)
    start = key_rows.shape[0] - own_len
    key_rows[start:, :] = own_key[...]
    value_rows[start:, :] = own_value[...]
    transpose_rows(key_rows, keys_t)
    for cols in tiles_of(width):
        forward_tile(
            cols, key_rows, value_rows, q_rows[cols, :], g_rows[cols, :],
            scores, expo, grad_prob, stats, own_len, comp_len,
        )


def near_kernel(
    column, q_rows, g_rows,
    keys_t, expo, grad_prob, stats,
    key_rows, value_rows, scores,
):
    copy_column(column, key_rows, value_rows, 0)
    transpose_rows(key_rows, keys_t)
    for cols in tiles_of(q_rows.shape[0]):
        forward_tile(
            cols, key_rows, value_rows, q_rows[cols, :], g_rows[cols, :],
            scores, expo, grad_prob, stats, 0, 0,
        )


def last_kernel(
    place, columns_0, columns_1, columns_2, columns_3, mine, mask, q_rows, g_rows,
    keys_t0, expo_0, grad_prob_0, stats_0, keys_t1, expo_1, grad_prob_1, stats_1,
    keys_t2, expo_2, grad_prob_2, stats_2,
    query_grad, own_key_grad, own_value_grad, prompt_grads,
    key_rows, value_rows, keys_t3, expo_3, grad_prob_3, stats_3, scores, grad_score, key_acc, value_acc, dq_t,
):
    columns = (columns_0, columns_1, columns_2, columns_3)
    along_x, along_z = len(columns), columns_0.shape[0]
    block = columns_0.shape[1] - META
    half = block // 2
    width = q_rows.shape[0]
    comp_len = mask.shape[1]
    members = along_x * along_z

    length_sum = jnp.zeros((1, 128), jnp.float32)
    reward_sum = jnp.zeros((1, 128), jnp.float32)
    square_sum = jnp.zeros((1, 128), jnp.float32)
    for column in columns:
        for i in range(along_z):
            meta = column[i, block:block + META, :].astype(jnp.float32)
            reward = meta[1:2, :]
            length_sum += meta[0:1, :]
            reward_sum += reward
            square_sum += reward * reward
    own_meta = mine[block:block + META, :].astype(jnp.float32)
    reward_mean = reward_sum / members
    variance = square_sum / members - reward_mean * reward_mean
    advantage = (own_meta[1:2, :] - reward_mean) / jnp.sqrt(variance + 1.0)
    positions = lax.broadcasted_iota(jnp.int32, (1, comp_len), 1).astype(jnp.float32)
    valid = jnp.where(positions < own_meta[0:1, :], mask[...].astype(jnp.float32), 0.0)
    weights = advantage * valid * (members * comp_len / length_sum)
    weight_row = jnp.concatenate([weights] * (TILE // comp_len), axis=1)

    copy_column(columns[3], key_rows, value_rows, 0)
    transpose_rows(key_rows, keys_t3)
    groups = (
        (keys_t0, expo_0, grad_prob_0, stats_0),
        (keys_t1, expo_1, grad_prob_1, stats_1),
        (keys_t2, expo_2, grad_prob_2, stats_2),
        (keys_t3, expo_3, grad_prob_3, stats_3),
    )
    for j, cols in enumerate(tiles_of(width)):
        q_tile = q_rows[cols, :]
        g_tile = g_rows[cols, :]
        forward_tile(cols, key_rows, value_rows, q_tile, g_tile, scores, expo_3, grad_prob_3, stats_3, 0, 0)
        tops = [stats[0:1, cols] for *_, stats in groups]
        top = jnp.maximum(jnp.maximum(tops[0], tops[1]), jnp.maximum(tops[2], tops[3]))
        shares = [jnp.exp2((t - top) * (SCALE * LOG2E)) for t in tops]
        sums = sum(share * stats[8:16, cols] for share, (*_, stats) in zip(shares, groups))
        dots = sum(share * stats[16:24, cols] for share, (*_, stats) in zip(shares, groups))
        inverse = 1.0 / jnp.sum(sums, axis=0, keepdims=True)
        delta = jnp.sum(dots, axis=0, keepdims=True) * inverse
        factor = weight_row * inverse
        dq = None
        start = 0
        for share, (keys_t, expo, grad_prob, _) in zip(shares, groups):
            part = factor * share
            column = jnp.concatenate(
                [jnp.broadcast_to(part[:, k:k + 128], (128, 128)).T for k in range(0, TILE, 128)], axis=0
            )
            g_scaled = (g_tile.astype(jnp.float32) * column).astype(jnp.bfloat16)
            q_scaled = (q_tile.astype(jnp.float32) * (column * SCALE)).astype(jnp.bfloat16)
            total = keys_t.shape[1]
            chunk = 512 if total % 512 == 0 else total // 2
            for i in range(0, total, chunk):
                rows = slice(i, i + chunk)
                out = slice(start + i, start + i + chunk)
                e = expo[rows, cols]
                ds = (e.astype(jnp.float32) * (grad_prob[rows, cols] - delta)).astype(jnp.bfloat16)
                grad_score[out, :] = ds
                dv = jnp.dot(e, g_scaled, preferred_element_type=jnp.float32)
                dk = jnp.dot(ds, q_scaled, preferred_element_type=jnp.float32)
                value_acc[out, :] = dv if j == 0 else value_acc[out, :] + dv
                key_acc[out, :] = dk if j == 0 else key_acc[out, :] + dk
            some = jnp.dot(keys_t[...], grad_score[start:start + total, :], preferred_element_type=jnp.float32)
            some = some * (part * SCALE)
            dq = some if dq is None else dq + some
            start += total
        dq_t[j] = dq

    for h in range(width // HEAD_DIM):
        j, k = divmod(h * HEAD_DIM, TILE)
        query_grad[:, h * HEAD_DIM:(h + 1) * HEAD_DIM] = dq_t[j, :, k:k + HEAD_DIM].T
    own_start = along_z * half
    own_len = own_key_grad.shape[0]
    own_key_grad[...] = key_acc[own_start:own_start + own_len, :]
    own_value_grad[...] = value_acc[own_start:own_start + own_len, :]
    starts = [0] + [own_start + own_len + k * own_start for k in range(along_x - 1)]
    for start, shift in zip(starts, SHIFTS):
        target = lax.rem(place[0] + (along_x - shift), along_x)
        for i in range(along_z):
            rows = slice(start + i * half, start + (i + 1) * half)
            prompt_grads[target, i, :half, :] = key_acc[rows, :].astype(jnp.bfloat16)
            prompt_grads[target, i, half:, :] = value_acc[rows, :].astype(jnp.bfloat16)


def forward_outputs(total, width):
    return (
        jax.ShapeDtypeStruct((HEAD_DIM, total), jnp.bfloat16),
        jax.ShapeDtypeStruct((total, width), jnp.bfloat16),
        jax.ShapeDtypeStruct((total, width), jnp.float32),
        jax.ShapeDtypeStruct((24, width), jnp.float32),
    )


def scratch(total):
    return [
        pltpu.VMEM((total, HEAD_DIM), jnp.bfloat16),
        pltpu.VMEM((total, HEAD_DIM), jnp.bfloat16),
    ]


VMEM = pl.BlockSpec(memory_space=pltpu.VMEM)


def params(mebibytes):
    return pltpu.CompilerParams(vmem_limit_bytes=mebibytes * 1024 * 1024)


def cost(total, width, passes):
    units = total * width
    return pl.CostEstimate(flops=2 * HEAD_DIM * units * passes, bytes_accessed=0, transcendentals=units)


def own_forward(column, own_key, own_value, queries, grads):
    width = queries.shape[1]
    total = column.shape[0] * (column.shape[1] - META) // 2 + own_key.shape[0]
    rows = jax.ShapeDtypeStruct((width, HEAD_DIM), jnp.bfloat16)
    outs = (rows, rows, *forward_outputs(total, width))
    return pl.pallas_call(
        own_kernel,
        out_shape=outs,
        in_specs=[VMEM] * 5,
        out_specs=(VMEM,) * len(outs),
        scratch_shapes=[*scratch(total), pltpu.VMEM((total, TILE), jnp.float32)],
        compiler_params=params(24),
        cost_estimate=cost(total, width, 2),
        name="own_forward",
    )(column, own_key, own_value, queries, grads)


def near_forward(column, q_rows, g_rows):
    width = q_rows.shape[0]
    total = column.shape[0] * (column.shape[1] - META) // 2
    outs = forward_outputs(total, width)
    return pl.pallas_call(
        near_kernel,
        out_shape=outs,
        in_specs=[VMEM] * 3,
        out_specs=(VMEM,) * len(outs),
        scratch_shapes=[*scratch(total), pltpu.VMEM((total, TILE), jnp.float32)],
        compiler_params=params(24),
        cost_estimate=cost(total, width, 2),
        name="near_forward",
    )(column, q_rows, g_rows)


def last_and_backward(place, columns, mine, mask, q_rows, g_rows, own_state, near_state):
    width = q_rows.shape[0]
    along_z, packed, dim = columns[0].shape
    block = packed - META
    comp_len = mask.shape[1]
    column_rows = along_z * block // 2
    own_len = own_state[0].shape[1] - column_rows
    total = len(columns) * column_rows + own_len
    f32, bf16 = jnp.float32, jnp.bfloat16
    state = [*own_state, *near_state]
    return pl.pallas_call(
        last_kernel,
        out_shape=(
            jax.ShapeDtypeStruct((comp_len, width), f32),
            jax.ShapeDtypeStruct((own_len, dim), f32),
            jax.ShapeDtypeStruct((own_len, dim), f32),
            jax.ShapeDtypeStruct((len(columns), along_z, block, dim), bf16),
        ),
        in_specs=[pl.BlockSpec(memory_space=pltpu.SMEM)] + [VMEM] * (len(columns) + 4 + len(state)),
        out_specs=(VMEM,) * 4,
        scratch_shapes=[
            *scratch(column_rows),
            *[pltpu.VMEM(out.shape, out.dtype) for out in forward_outputs(column_rows, width)],
            pltpu.VMEM((column_rows, TILE), f32),
            pltpu.VMEM((total, TILE), bf16),
            pltpu.VMEM((total, dim), f32),
            pltpu.VMEM((total, dim), f32),
            pltpu.VMEM((width // TILE, dim, TILE), f32),
        ],
        compiler_params=params(36),
        cost_estimate=cost(total, width, 4),
        name="last_and_backward",
    )(place, *columns, mine, mask, q_rows, g_rows, *state)


def shifted(column, shift):
    size = lax.axis_size("gx")
    return lax.ppermute(column, "gx", [(i, (i + shift) % size) for i in range(size)])


def body(queries, comp_keys, comp_values, prompt_keys, prompt_values, out_grad, lengths, loss_mask, buckets):
    row = lax.broadcasted_iota(jnp.int32, (META, prompt_keys.shape[1]), 0)
    meta = jnp.where(row == 0, lengths[0], jnp.where(row == 1, buckets[0], 0)).astype(jnp.bfloat16)
    mine = jnp.concatenate([prompt_keys, prompt_values, meta], axis=0)
    column = lax.all_gather(mine, "gz")
    columns = [column] + [None] * 3
    for k in (3, 1, 2):
        columns[k] = shifted(column, SHIFTS[k])
    q_rows, g_rows, *own_state = own_forward(column, comp_keys[0], comp_values[0], queries[0], out_grad[0])
    near_state = [*near_forward(columns[1], q_rows, g_rows), *near_forward(columns[2], q_rows, g_rows)]
    place = lax.axis_index("gx").astype(jnp.int32)[None]
    query_grad, own_key_grad, own_value_grad, prompt_grads = last_and_backward(
        place, columns, mine, loss_mask, q_rows, g_rows, own_state, near_state
    )
    terms = lax.all_to_all(prompt_grads, "gx", 0, 0)
    partial = jnp.sum(terms.astype(jnp.float32), axis=0).astype(jnp.bfloat16)
    terms = lax.all_to_all(jnp.stack([partial[i] for i in Z_ORDER]), "gz", 0, 0, axis_index_groups=[Z_ORDER])
    owned = jnp.sum(terms.astype(jnp.float32), axis=0)
    half = owned.shape[0] // 2
    return (
        query_grad[None],
        own_key_grad[None],
        own_value_grad[None],
        owned[:half],
        owned[half:],
    )


def solution(mesh):
    dp, group, tensor = (mesh.shape[name] for name in ("dp", "group", "tensor"))
    along_z = 4
    split = jax.sharding.Mesh(
        mesh.devices.reshape(dp, group // along_z, along_z, tensor), ("dp", "gx", "gz", "tensor")
    )
    rows = ("dp", "gx", "gz")
    return jax.shard_map(
        body,
        mesh=split,
        in_specs=(
            P(rows, None, "tensor"),
            P(rows, None, "tensor"),
            P(rows, None, "tensor"),
            P(rows, "tensor"),
            P(rows, "tensor"),
            P(rows, None, "tensor"),
            P(rows),
            P(rows, None),
            P(rows),
        ),
        out_specs=(
            P(rows, None, "tensor"),
            P(rows, None, "tensor"),
            P(rows, None, "tensor"),
            P(rows, "tensor"),
            P(rows, "tensor"),
        ),
        check_vma=False,
    )
```

time: 90 us -> 88.3 us (0.981)
  the two profiles are of different devices: /device:TPU:56 before, /device:TPU:40 now
where the time goes in v3:
time: 88.3 us; the launch traced here: 87.8 us
  blocking collectives  58 us (66%)
  starting transfers between devices  10.8 us (12%)
  Pallas kernels  8.5 us (10%)
  local copies, waits for them, and re-layouts  4.09 us (5%)
  waiting for transfers between devices  3.19 us (4%)
  between operations  2.06 us (2%)
  other arithmetic  1.16 us (1%)
    all_gather x1, blocking collectives, body(): column = lax.all_gather(mine, 'gz')  26.1 us
    all_to_all x1, blocking collectives, body(): lax.all_to_all(jnp.stack([partial[i] for i in Z_ORDER]), 'gz', 0, 0, axis...  18.1 us
    all_to_all x1, blocking collectives, body(): terms = lax.all_to_all(prompt_grads, 'gx', 0, 0)  13.8 us
    ppermute x3, starting transfers between devices, shifted(): lax.ppermute(column, 'gx', [(i, (i + shift) % size) for i in range(size)])  10.8 us
    pallas_call x1, Pallas kernels, last_and_backward(): pl.pallas_call(last_kernel, out_shape=(jax.ShapeDtypeStruct((comp_len, wi...  5.59 us
    unnamed x10, local copies, waits for them, and re-layouts  3.41 us
    ppermute x3, waiting for transfers between devices, shifted(): lax.ppermute(column, 'gx', [(i, (i + shift) % size) for i in range(size)])  3.19 us
  transfers between devices with their start and end apart: 3, of which 1 were waited for; matrix products, arithmetic and copies ran while one was open for 0% of the time, Pallas kernels for 3%

profile of v3, /device:TPU:40, one launch (start us, length us, event | category | flops | bytes accessed | tf_op | source)
XLA Modules:
  0.0 87.8 jit_solution(16089112239669802228)
XLA Ops:
  0.6 0.0 copy-start
  2.0 0.1 select_convert_fusion
  2.0 0.8 pad_maximum_fusion.1.mine
  2.8 26.1 %all-gather = bf16[1088,128]{1,0:T(8,128)(2,1)S(1)} all-gather(bf16[272,128]{1,0:T(8,128)(2,1)S(1)} %pad_maximum_fusion.1.mine), channel_id=2, replica_groups=mesh['dp'=4,'gx'=4,'gz'=4,'tensor'=8] {'gz'}, dimensions={0}, use_global_device_ids=true | all-gather | bytes 348160 | tf_op jit(solution)/shard_map/all_gather | solution.py:311
  28.9 4.7 %collective-permute-start.1 = (bf16[4,272,128]{2,1,0:T(8,128)(2,1)S(1)}, bf16[4,272,128]{2,1,0:T(8,128)(2,1)S(1)}, u32[]{:S(2)}, u32[]{:S(2)}) collective-permute-start(bf16[4,272,128]{2,1,0:T(8,128)(2,1)S(1)} %bitcast.13), channel_id=1, source_target_pairs={{0,96},{32,0},{64,32},{96,64},{1,97},{33,1},{65,33},{97,65},{2,98}... | collective-permute-start | bytes 835592 | tf_op jit(solution)/shard_map/ppermute | solution.py:304
  33.6 1.9 %collective-permute-start = (bf16[4,272,128]{2,1,0:T(8,128)(2,1)S(1)}, bf16[4,272,128]{2,1,0:T(8,128)(2,1)S(1)}, u32[]{:S(2)}, u32[]{:S(2)}) collective-permute-start(bf16[4,272,128]{2,1,0:T(8,128)(2,1)S(1)} %bitcast.14), channel_id=1, source_target_pairs={{0,32},{32,64},{64,96},{96,0},{1,33},{33,65},{65,97},{97,1},{2,34}... | collective-permute-start | bytes 835592 | tf_op jit(solution)/shard_map/ppermute | solution.py:304
  35.5 4.2 %collective-permute-start.2 = (bf16[4,272,128]{2,1,0:T(8,128)(2,1)S(1)}, bf16[4,272,128]{2,1,0:T(8,128)(2,1)S(1)}, u32[]{:S(2)}, u32[]{:S(2)}) collective-permute-start(bf16[4,272,128]{2,1,0:T(8,128)(2,1)S(1)} %bitcast.15), channel_id=1, source_target_pairs={{0,64},{32,96},{64,0},{96,32},{1,65},{33,97},{65,1},{97,33},{2,66}... | collective-permute-start | bytes 835592 | tf_op jit(solution)/shard_map/ppermute | solution.py:304
  39.7 0.0 copy-start.1
  39.8 0.9 %copy-done.1 = bf16[1,128,1024]{2,1,0:T(8,128)(2,1)S(1)} copy-done((bf16[1,128,1024]{2,1,0:T(8,128)(2,1)S(1)}, bf16[1,128,1024]{2,1,0:T(8,128)(2,1)}, u32[]{:S(2)}) %copy-start.1) | copy-done | bytes 262168
  40.7 0.0 copy-start.2
  40.7 0.9 %copy-done.2 = bf16[1,128,1024]{2,1,0:T(8,128)(2,1)S(1)} copy-done((bf16[1,128,1024]{2,1,0:T(8,128)(2,1)S(1)}, bf16[1,128,1024]{2,1,0:T(8,128)(2,1)}, u32[]{:S(2)}) %copy-start.2) | copy-done | bytes 262168
  41.6 0.0 copy-start.3
  41.6 0.8 copy-done.3
  42.4 0.0 copy-start.4
  42.4 0.8 copy-done.4
  43.2 1.2 %own_forward.1 = (bf16[1024,128]{1,0:T(8,128)(2,1)S(1)}, bf16[1024,128]{1,0:T(8,128)(2,1)S(1)}, bf16[128,640]{1,0:T(8,128)(2,1)S(1)}, bf16[640,1024]{1,0:T(8,128...) custom-call(bf16[4,272,128]{2,1,0:T(8,128)(2,1)S(1)} %bitcast.16, bf16[128,128]{1,0:T(8,128)(2,1)S(1)} %bitcast.20, ...), custom_call_target="tpu_custom_call" | custom-call | flops 335544320 | tf_op jit(solution)/shard_map/own_forward/pallas_call | solution.py:239
  44.3 0.0 collective-permute-done.1.column.columns_2
  44.4 0.9 near_forward.3
  45.2 3.2 %collective-permute-done.column.columns_1 = bf16[4,272,128]{2,1,0:T(8,128)(2,1)S(1)} collective-permute-done((bf16[4,272,128]{2,1,0:T(8,128)(2,1)S(1)}, bf16[4,272,128]{2,1,0:T(8,128)(2,1)S(1)}, u32[]{:S(2)}, u32[]{:S(2)}) %collective-permute-start) | collective-permute-done | bytes 278560 | tf_op jit(solution)/shard_map/ppermute | solution.py:304
  48.4 0.9 near_forward.2
  49.3 0.0 collective-permute-done.2.columns_3
  49.3 0.0 copy-done
  49.3 5.6 %last_and_backward.1 = (f32[128,1024]{1,0:T(8,128)}, f32[128,128]{1,0:T(8,128)}, f32[128,128]{1,0:T(8,128)}, bf16[4,4,256,128]{3,2,1,0:T(8,128)(2,1)S(1)}) custom-call(s32[1]{0:T(128)} %bitcast.place, bf16[4,272,128]{2,1,0:T(8,128)(2,1)S(1)} %bitcast.17, bf16[4,272,128]{2,1,0:T(8,128)(2,1)S(1)} %collective-permute-done.column.columns_1, ...), custom_call_target="tpu_custom_call" | custom-call | flops 2281701376 | tf_op jit(solution)/shard_map/last_and_backward/pallas_call | solution.py:277
  54.9 13.8 %all_to_all.10 = bf16[4,4,256,128]{3,2,1,0:T(8,128)(2,1)S(1)} all-to-all(bf16[4,4,256,128]{3,2,1,0:T(8,128)(2,1)S(1)} %get-tuple-element.40), channel_id=1, replica_groups=mesh['dp'=4,'gx'=4,'gz'=4,'tensor'=8] {'gx'}, dimensions={0} | all-to-all | bytes 2097152 | tf_op jit(solution)/shard_map/all_to_all | solution.py:321
  68.7 0.2 reduce_sum.21
  69.0 18.1 %all_to_all.11 = bf16[4,256,128]{2,1,0:T(8,128)(2,1)S(1)} all-to-all(bf16[4,256,128]{2,1,0:T(8,128)(2,1)S(1)} %pad_maximum_fusion), channel_id=1, replica_groups={{16,8,0,24},{17,9,1,25},{18,10,2,26},{19,11,3,27},{20,12,4,28},{21,13,5..., dimensions={0} | all-to-all | bytes 524288 | tf_op jit(solution)/shard_map/all_to_all | solution.py:323
  87.1 0.7 fusion.1
  (5 shorter events, 0.1 us)
Async XLA Ops:
  0.6 48.7 %copy-start = (s32[1,128]{1,0:T(1,128)S(1)}, s32[1,128]{1,0:T(1,128)}, u32[]{:S(2)}) copy-start(s32[1,128]{1,0:T(1,128)} %mask.1) | copy-start | bytes 1540
  28.9 15.4 %collective-permute-start.1 = (bf16[4,272,128]{2,1,0:T(8,128)(2,1)S(1)}, bf16[4,272,128]{2,1,0:T(8,128)(2,1)S(1)}, u32[]{:S(2)}, u32[]{:S(2)}) collective-permute-start(bf16[4,272,128]{2,1,0:T(8,128)(2,1)S(1)} %bitcast.13), channel_id=1, source_target_pairs={{0,96},{32,0},{64,32},{96,64},{1,97},{33,1},{65,33},{97,65},{2,98}... | collective-permute-start | bytes 835592 | tf_op jit(solution)/shard_map/ppermute | solution.py:304
  33.6 14.8 %collective-permute-start = (bf16[4,272,128]{2,1,0:T(8,128)(2,1)S(1)}, bf16[4,272,128]{2,1,0:T(8,128)(2,1)S(1)}, u32[]{:S(2)}, u32[]{:S(2)}) collective-permute-start(bf16[4,272,128]{2,1,0:T(8,128)(2,1)S(1)} %bitcast.14), channel_id=1, source_target_pairs={{0,32},{32,64},{64,96},{96,0},{1,33},{33,65},{65,97},{97,1},{2,34}... | collective-permute-start | bytes 835592 | tf_op jit(solution)/shard_map/ppermute | solution.py:304
  35.5 13.8 %collective-permute-start.2 = (bf16[4,272,128]{2,1,0:T(8,128)(2,1)S(1)}, bf16[4,272,128]{2,1,0:T(8,128)(2,1)S(1)}, u32[]{:S(2)}, u32[]{:S(2)}) collective-permute-start(bf16[4,272,128]{2,1,0:T(8,128)(2,1)S(1)} %bitcast.15), channel_id=1, source_target_pairs={{0,64},{32,96},{64,0},{96,32},{1,65},{33,97},{65,1},{97,33},{2,66}... | collective-permute-start | bytes 835592 | tf_op jit(solution)/shard_map/ppermute | solution.py:304
  39.7 1.0 %copy-start.1 = (bf16[1,128,1024]{2,1,0:T(8,128)(2,1)S(1)}, bf16[1,128,1024]{2,1,0:T(8,128)(2,1)}, u32[]{:S(2)}) copy-start(bf16[1,128,1024]{2,1,0:T(8,128)(2,1)} %param.9) | copy-start | bytes 786436
  40.7 0.9 %copy-start.2 = (bf16[1,128,1024]{2,1,0:T(8,128)(2,1)S(1)}, bf16[1,128,1024]{2,1,0:T(8,128)(2,1)}, u32[]{:S(2)}) copy-start(bf16[1,128,1024]{2,1,0:T(8,128)(2,1)} %param.14) | copy-start | bytes 786436
  41.6 0.8 copy-start.3
  42.4 0.8 copy-start.4

commit v4 on v3

--- a/solution.py
+++ b/solution.py
@@ -148,10 +148,14 @@
         (keys_t2, expo_2, grad_prob_2, stats_2),
         (keys_t3, expo_3, grad_prob_3, stats_3),
     )
+    for cols in tiles_of(width):
+        forward_tile(
+            cols, key_rows, value_rows, q_rows[cols, :], g_rows[cols, :],
+            scores, expo_3, grad_prob_3, stats_3, 0, 0,
+        )
     for j, cols in enumerate(tiles_of(width)):
         q_tile = q_rows[cols, :]
         g_tile = g_rows[cols, :]
-        forward_tile(cols, key_rows, value_rows, q_tile, g_tile, scores, expo_3, grad_prob_3, stats_3, 0, 0)
         tops = [stats[0:1, cols] for *_, stats in groups]
         top = jnp.maximum(jnp.maximum(tops[0], tops[1]), jnp.maximum(tops[2], tops[3]))
         shares = [jnp.exp2((t - top) * (SCALE * LOG2E)) for t in tops]

time: 88.3 us -> 88.1 us (level)
  the two profiles are of different devices: /device:TPU:40 before, /device:TPU:48 now
where the time goes in v4:
time: 88.1 us; the launch traced here: 87.5 us
  blocking collectives  58 us (66%)
  starting transfers between devices  10.8 us (12%)
  Pallas kernels  8.24 us (9%)
  local copies, waits for them, and re-layouts  4.09 us (5%)
  waiting for transfers between devices  3.19 us (4%)
  between operations  2.06 us (2%)
  other arithmetic  1.16 us (1%)
    all_gather x1, blocking collectives, body(): column = lax.all_gather(mine, 'gz')  26.1 us
    all_to_all x1, blocking collectives, body(): lax.all_to_all(jnp.stack([partial[i] for i in Z_ORDER]), 'gz', 0, 0, axis...  18.1 us
    all_to_all x1, blocking collectives, body(): terms = lax.all_to_all(prompt_grads, 'gx', 0, 0)  13.8 us
    ppermute x3, starting transfers between devices, shifted(): lax.ppermute(column, 'gx', [(i, (i + shift) % size) for i in range(size)])  10.8 us
    pallas_call x1, Pallas kernels, last_and_backward(): pl.pallas_call(last_kernel, out_shape=(jax.ShapeDtypeStruct((comp_len, wi...  5.33 us
    unnamed x10, local copies, waits for them, and re-layouts  3.41 us
    ppermute x3, waiting for transfers between devices, shifted(): lax.ppermute(column, 'gx', [(i, (i + shift) % size) for i in range(size)])  3.19 us
  transfers between devices with their start and end apart: 3, of which 1 were waited for; matrix products, arithmetic and copies ran while one was open for 0% of the time, Pallas kernels for 3%

profile of v4, /device:TPU:48, one launch (start us, length us, event | category | flops | bytes accessed | tf_op | source)
XLA Modules:
  0.0 87.5 jit_solution(7606642737961699651)
XLA Ops:
  0.6 0.0 copy-start
  2.0 0.1 select_convert_fusion
  2.0 0.8 pad_maximum_fusion.1.mine
  2.8 26.1 %all-gather = bf16[1088,128]{1,0:T(8,128)(2,1)S(1)} all-gather(bf16[272,128]{1,0:T(8,128)(2,1)S(1)} %pad_maximum_fusion.1.mine), channel_id=2, replica_groups=mesh['dp'=4,'gx'=4,'gz'=4,'tensor'=8] {'gz'}, dimensions={0}, use_global_device_ids=true | all-gather | bytes 348160 | tf_op jit(solution)/shard_map/all_gather | solution.py:315
  28.9 4.7 %collective-permute-start.1 = (bf16[4,272,128]{2,1,0:T(8,128)(2,1)S(1)}, bf16[4,272,128]{2,1,0:T(8,128)(2,1)S(1)}, u32[]{:S(2)}, u32[]{:S(2)}) collective-permute-start(bf16[4,272,128]{2,1,0:T(8,128)(2,1)S(1)} %bitcast.13), channel_id=1, source_target_pairs={{0,96},{32,0},{64,32},{96,64},{1,97},{33,1},{65,33},{97,65},{2,98}... | collective-permute-start | bytes 835592 | tf_op jit(solution)/shard_map/ppermute | solution.py:308
  33.6 1.9 %collective-permute-start = (bf16[4,272,128]{2,1,0:T(8,128)(2,1)S(1)}, bf16[4,272,128]{2,1,0:T(8,128)(2,1)S(1)}, u32[]{:S(2)}, u32[]{:S(2)}) collective-permute-start(bf16[4,272,128]{2,1,0:T(8,128)(2,1)S(1)} %bitcast.14), channel_id=1, source_target_pairs={{0,32},{32,64},{64,96},{96,0},{1,33},{33,65},{65,97},{97,1},{2,34}... | collective-permute-start | bytes 835592 | tf_op jit(solution)/shard_map/ppermute | solution.py:308
  35.5 4.2 %collective-permute-start.2 = (bf16[4,272,128]{2,1,0:T(8,128)(2,1)S(1)}, bf16[4,272,128]{2,1,0:T(8,128)(2,1)S(1)}, u32[]{:S(2)}, u32[]{:S(2)}) collective-permute-start(bf16[4,272,128]{2,1,0:T(8,128)(2,1)S(1)} %bitcast.15), channel_id=1, source_target_pairs={{0,64},{32,96},{64,0},{96,32},{1,65},{33,97},{65,1},{97,33},{2,66}... | collective-permute-start | bytes 835592 | tf_op jit(solution)/shard_map/ppermute | solution.py:308
  39.7 0.0 copy-start.1
  39.8 0.9 %copy-done.1 = bf16[1,128,1024]{2,1,0:T(8,128)(2,1)S(1)} copy-done((bf16[1,128,1024]{2,1,0:T(8,128)(2,1)S(1)}, bf16[1,128,1024]{2,1,0:T(8,128)(2,1)}, u32[]{:S(2)}) %copy-start.1) | copy-done | bytes 262168
  40.7 0.0 copy-start.2
  40.7 0.9 %copy-done.2 = bf16[1,128,1024]{2,1,0:T(8,128)(2,1)S(1)} copy-done((bf16[1,128,1024]{2,1,0:T(8,128)(2,1)S(1)}, bf16[1,128,1024]{2,1,0:T(8,128)(2,1)}, u32[]{:S(2)}) %copy-start.2) | copy-done | bytes 262168
  41.6 0.0 copy-start.3
  41.6 0.8 copy-done.3
  42.4 0.0 copy-start.4
  42.4 0.8 copy-done.4
  43.2 1.2 %own_forward.1 = (bf16[1024,128]{1,0:T(8,128)(2,1)S(1)}, bf16[1024,128]{1,0:T(8,128)(2,1)S(1)}, bf16[128,640]{1,0:T(8,128)(2,1)S(1)}, bf16[640,1024]{1,0:T(8,128...) custom-call(bf16[4,272,128]{2,1,0:T(8,128)(2,1)S(1)} %bitcast.16, bf16[128,128]{1,0:T(8,128)(2,1)S(1)} %bitcast.20, ...), custom_call_target="tpu_custom_call" | custom-call | flops 335544320 | tf_op jit(solution)/shard_map/own_forward/pallas_call | solution.py:243
  44.3 0.0 collective-permute-done.1.column.columns_2
  44.4 0.9 near_forward.3
  45.2 3.2 %collective-permute-done.column.columns_1 = bf16[4,272,128]{2,1,0:T(8,128)(2,1)S(1)} collective-permute-done((bf16[4,272,128]{2,1,0:T(8,128)(2,1)S(1)}, bf16[4,272,128]{2,1,0:T(8,128)(2,1)S(1)}, u32[]{:S(2)}, u32[]{:S(2)}) %collective-permute-start) | collective-permute-done | bytes 278560 | tf_op jit(solution)/shard_map/ppermute | solution.py:308
  48.4 0.9 near_forward.2
  49.3 0.0 collective-permute-done.2.columns_3
  49.3 0.0 copy-done
  49.3 5.3 %last_and_backward.1 = (f32[128,1024]{1,0:T(8,128)}, f32[128,128]{1,0:T(8,128)}, f32[128,128]{1,0:T(8,128)}, bf16[4,4,256,128]{3,2,1,0:T(8,128)(2,1)S(1)}) custom-call(s32[1]{0:T(128)} %bitcast.place, bf16[4,272,128]{2,1,0:T(8,128)(2,1)S(1)} %bitcast.17, bf16[4,272,128]{2,1,0:T(8,128)(2,1)S(1)} %collective-permute-done.column.columns_1, ...), custom_call_target="tpu_custom_call" | custom-call | flops 2281701376 | tf_op jit(solution)/shard_map/last_and_backward/pallas_call | solution.py:281
  54.6 13.8 %all_to_all.10 = bf16[4,4,256,128]{3,2,1,0:T(8,128)(2,1)S(1)} all-to-all(bf16[4,4,256,128]{3,2,1,0:T(8,128)(2,1)S(1)} %get-tuple-element.40), channel_id=1, replica_groups=mesh['dp'=4,'gx'=4,'gz'=4,'tensor'=8] {'gx'}, dimensions={0} | all-to-all | bytes 2097152 | tf_op jit(solution)/shard_map/all_to_all | solution.py:325
  68.4 0.2 reduce_sum.21
  68.7 18.1 %all_to_all.11 = bf16[4,256,128]{2,1,0:T(8,128)(2,1)S(1)} all-to-all(bf16[4,256,128]{2,1,0:T(8,128)(2,1)S(1)} %pad_maximum_fusion), channel_id=1, replica_groups={{16,8,0,24},{17,9,1,25},{18,10,2,26},{19,11,3,27},{20,12,4,28},{21,13,5..., dimensions={0} | all-to-all | bytes 524288 | tf_op jit(solution)/shard_map/all_to_all | solution.py:327
  86.9 0.7 fusion.1
  (5 shorter events, 0.1 us)
Async XLA Ops:
  0.6 48.7 %copy-start = (s32[1,128]{1,0:T(1,128)S(1)}, s32[1,128]{1,0:T(1,128)}, u32[]{:S(2)}) copy-start(s32[1,128]{1,0:T(1,128)} %mask.1) | copy-start | bytes 1540
  28.9 15.4 %collective-permute-start.1 = (bf16[4,272,128]{2,1,0:T(8,128)(2,1)S(1)}, bf16[4,272,128]{2,1,0:T(8,128)(2,1)S(1)}, u32[]{:S(2)}, u32[]{:S(2)}) collective-permute-start(bf16[4,272,128]{2,1,0:T(8,128)(2,1)S(1)} %bitcast.13), channel_id=1, source_target_pairs={{0,96},{32,0},{64,32},{96,64},{1,97},{33,1},{65,33},{97,65},{2,98}... | collective-permute-start | bytes 835592 | tf_op jit(solution)/shard_map/ppermute | solution.py:308
  33.6 14.8 %collective-permute-start = (bf16[4,272,128]{2,1,0:T(8,128)(2,1)S(1)}, bf16[4,272,128]{2,1,0:T(8,128)(2,1)S(1)}, u32[]{:S(2)}, u32[]{:S(2)}) collective-permute-start(bf16[4,272,128]{2,1,0:T(8,128)(2,1)S(1)} %bitcast.14), channel_id=1, source_target_pairs={{0,32},{32,64},{64,96},{96,0},{1,33},{33,65},{65,97},{97,1},{2,34}... | collective-permute-start | bytes 835592 | tf_op jit(solution)/shard_map/ppermute | solution.py:308
  35.5 13.8 %collective-permute-start.2 = (bf16[4,272,128]{2,1,0:T(8,128)(2,1)S(1)}, bf16[4,272,128]{2,1,0:T(8,128)(2,1)S(1)}, u32[]{:S(2)}, u32[]{:S(2)}) collective-permute-start(bf16[4,272,128]{2,1,0:T(8,128)(2,1)S(1)} %bitcast.15), channel_id=1, source_target_pairs={{0,64},{32,96},{64,0},{96,32},{1,65},{33,97},{65,1},{97,33},{2,66}... | collective-permute-start | bytes 835592 | tf_op jit(solution)/shard_map/ppermute | solution.py:308
  39.7 1.0 %copy-start.1 = (bf16[1,128,1024]{2,1,0:T(8,128)(2,1)S(1)}, bf16[1,128,1024]{2,1,0:T(8,128)(2,1)}, u32[]{:S(2)}) copy-start(bf16[1,128,1024]{2,1,0:T(8,128)(2,1)} %param.9) | copy-start | bytes 786436
  40.7 0.9 %copy-start.2 = (bf16[1,128,1024]{2,1,0:T(8,128)(2,1)S(1)}, bf16[1,128,1024]{2,1,0:T(8,128)(2,1)}, u32[]{:S(2)}) copy-start(bf16[1,128,1024]{2,1,0:T(8,128)(2,1)} %param.14) | copy-start | bytes 786436
  41.6 0.8 copy-start.3
  42.4 0.8 copy-start.4

commit v5 on v4

--- a/solution.py
+++ b/solution.py
@@ -325,14 +325,15 @@
     terms = lax.all_to_all(prompt_grads, "gx", 0, 0)
     partial = jnp.sum(terms.astype(jnp.float32), axis=0).astype(jnp.bfloat16)
     terms = lax.all_to_all(jnp.stack([partial[i] for i in Z_ORDER]), "gz", 0, 0, axis_index_groups=[Z_ORDER])
-    owned = jnp.sum(terms.astype(jnp.float32), axis=0)
-    half = owned.shape[0] // 2
+    half = terms.shape[1] // 2
+    owned_keys = jnp.sum(terms[:, :half].astype(jnp.float32), axis=0)
+    owned_values = jnp.sum(terms[:, half:].astype(jnp.float32), axis=0)
     return (
         query_grad[None],
         own_key_grad[None],
         own_value_grad[None],
-        owned[:half],
-        owned[half:],
+        owned_keys,
+        owned_values,
     )
 
 

time: 88.1 us -> 88 us (level)
  the two profiles are of different devices: /device:TPU:48 before, /device:TPU:56 now
where the time goes in v5:
time: 88 us; the launch traced here: 87.5 us
  blocking collectives  58 us (66%)
  starting transfers between devices  10.8 us (12%)
  Pallas kernels  8.24 us (9%)
  local copies, waits for them, and re-layouts  3.43 us (4%)
  waiting for transfers between devices  3.19 us (4%)
  between operations  2.05 us (2%)
  other arithmetic  1.81 us (2%)
    all_gather x1, blocking collectives, body(): column = lax.all_gather(mine, 'gz')  26.1 us
    all_to_all x1, blocking collectives, body(): lax.all_to_all(jnp.stack([partial[i] for i in Z_ORDER]), 'gz', 0, 0, axis...  18.1 us
    all_to_all x1, blocking collectives, body(): terms = lax.all_to_all(prompt_grads, 'gx', 0, 0)  13.8 us
    ppermute x3, starting transfers between devices, shifted(): lax.ppermute(column, 'gx', [(i, (i + shift) % size) for i in range(size)])  10.8 us
    pallas_call x1, Pallas kernels, last_and_backward(): pl.pallas_call(last_kernel, out_shape=(jax.ShapeDtypeStruct((comp_len, wi...  5.33 us
    unnamed x10, local copies, waits for them, and re-layouts  3.41 us
    ppermute x3, waiting for transfers between devices, shifted(): lax.ppermute(column, 'gx', [(i, (i + shift) % size) for i in range(size)])  3.19 us
  transfers between devices with their start and end apart: 3, of which 1 were waited for; matrix products, arithmetic and copies ran while one was open for 0% of the time, Pallas kernels for 3%

profile of v5, /device:TPU:56, one launch (start us, length us, event | category | flops | bytes accessed | tf_op | source)
XLA Modules:
  0.0 87.5 jit_solution(12443402576527675829)
XLA Ops:
  0.6 0.0 copy-start
  2.0 0.1 select_convert_fusion
  2.0 0.8 pad_maximum_fusion.1.mine
  2.8 26.1 %all-gather = bf16[1088,128]{1,0:T(8,128)(2,1)S(1)} all-gather(bf16[272,128]{1,0:T(8,128)(2,1)S(1)} %pad_maximum_fusion.1.mine), channel_id=2, replica_groups=mesh['dp'=4,'gx'=4,'gz'=4,'tensor'=8] {'gz'}, dimensions={0}, use_global_device_ids=true | all-gather | bytes 348160 | tf_op jit(solution)/shard_map/all_gather | solution.py:315
  28.9 4.7 %collective-permute-start.1 = (bf16[4,272,128]{2,1,0:T(8,128)(2,1)S(1)}, bf16[4,272,128]{2,1,0:T(8,128)(2,1)S(1)}, u32[]{:S(2)}, u32[]{:S(2)}) collective-permute-start(bf16[4,272,128]{2,1,0:T(8,128)(2,1)S(1)} %bitcast.13), channel_id=1, source_target_pairs={{0,96},{32,0},{64,32},{96,64},{1,97},{33,1},{65,33},{97,65},{2,98}... | collective-permute-start | bytes 835592 | tf_op jit(solution)/shard_map/ppermute | solution.py:308
  33.6 1.9 %collective-permute-start = (bf16[4,272,128]{2,1,0:T(8,128)(2,1)S(1)}, bf16[4,272,128]{2,1,0:T(8,128)(2,1)S(1)}, u32[]{:S(2)}, u32[]{:S(2)}) collective-permute-start(bf16[4,272,128]{2,1,0:T(8,128)(2,1)S(1)} %bitcast.14), channel_id=1, source_target_pairs={{0,32},{32,64},{64,96},{96,0},{1,33},{33,65},{65,97},{97,1},{2,34}... | collective-permute-start | bytes 835592 | tf_op jit(solution)/shard_map/ppermute | solution.py:308
  35.5 4.2 %collective-permute-start.2 = (bf16[4,272,128]{2,1,0:T(8,128)(2,1)S(1)}, bf16[4,272,128]{2,1,0:T(8,128)(2,1)S(1)}, u32[]{:S(2)}, u32[]{:S(2)}) collective-permute-start(bf16[4,272,128]{2,1,0:T(8,128)(2,1)S(1)} %bitcast.15), channel_id=1, source_target_pairs={{0,64},{32,96},{64,0},{96,32},{1,65},{33,97},{65,1},{97,33},{2,66}... | collective-permute-start | bytes 835592 | tf_op jit(solution)/shard_map/ppermute | solution.py:308
  39.7 0.0 copy-start.1
  39.8 0.9 %copy-done.1 = bf16[1,128,1024]{2,1,0:T(8,128)(2,1)S(1)} copy-done((bf16[1,128,1024]{2,1,0:T(8,128)(2,1)S(1)}, bf16[1,128,1024]{2,1,0:T(8,128)(2,1)}, u32[]{:S(2)}) %copy-start.1) | copy-done | bytes 262168
  40.7 0.0 copy-start.2
  40.7 0.9 %copy-done.2 = bf16[1,128,1024]{2,1,0:T(8,128)(2,1)S(1)} copy-done((bf16[1,128,1024]{2,1,0:T(8,128)(2,1)S(1)}, bf16[1,128,1024]{2,1,0:T(8,128)(2,1)}, u32[]{:S(2)}) %copy-start.2) | copy-done | bytes 262168
  41.6 0.0 copy-start.3
  41.6 0.8 copy-done.3
  42.4 0.0 copy-start.4
  42.4 0.8 copy-done.4
  43.2 1.2 %own_forward.1 = (bf16[1024,128]{1,0:T(8,128)(2,1)S(1)}, bf16[1024,128]{1,0:T(8,128)(2,1)S(1)}, bf16[128,640]{1,0:T(8,128)(2,1)S(1)}, bf16[640,1024]{1,0:T(8,128...) custom-call(bf16[4,272,128]{2,1,0:T(8,128)(2,1)S(1)} %bitcast.16, bf16[128,128]{1,0:T(8,128)(2,1)S(1)} %bitcast.20, ...), custom_call_target="tpu_custom_call" | custom-call | flops 335544320 | tf_op jit(solution)/shard_map/own_forward/pallas_call | solution.py:243
  44.3 0.0 collective-permute-done.1.column.columns_2
  44.4 0.9 near_forward.3
  45.2 3.2 %collective-permute-done.column.columns_1 = bf16[4,272,128]{2,1,0:T(8,128)(2,1)S(1)} collective-permute-done((bf16[4,272,128]{2,1,0:T(8,128)(2,1)S(1)}, bf16[4,272,128]{2,1,0:T(8,128)(2,1)S(1)}, u32[]{:S(2)}, u32[]{:S(2)}) %collective-permute-start) | collective-permute-done | bytes 278560 | tf_op jit(solution)/shard_map/ppermute | solution.py:308
  48.4 0.9 near_forward.2
  49.3 0.0 collective-permute-done.2.columns_3
  49.3 0.0 copy-done
  49.3 5.3 %last_and_backward.1 = (f32[128,1024]{1,0:T(8,128)}, f32[128,128]{1,0:T(8,128)}, f32[128,128]{1,0:T(8,128)}, bf16[4,4,256,128]{3,2,1,0:T(8,128)(2,1)S(1)}) custom-call(s32[1]{0:T(128)} %bitcast.place, bf16[4,272,128]{2,1,0:T(8,128)(2,1)S(1)} %bitcast.17, bf16[4,272,128]{2,1,0:T(8,128)(2,1)S(1)} %collective-permute-done.column.columns_1, ...), custom_call_target="tpu_custom_call" | custom-call | flops 2281701376 | tf_op jit(solution)/shard_map/last_and_backward/pallas_call | solution.py:281
  54.6 13.8 %all_to_all.10 = bf16[4,4,256,128]{3,2,1,0:T(8,128)(2,1)S(1)} all-to-all(bf16[4,4,256,128]{3,2,1,0:T(8,128)(2,1)S(1)} %get-tuple-element.40), channel_id=1, replica_groups=mesh['dp'=4,'gx'=4,'gz'=4,'tensor'=8] {'gx'}, dimensions={0} | all-to-all | bytes 2097152 | tf_op jit(solution)/shard_map/all_to_all | solution.py:325
  68.4 0.2 reduce_sum.30
  68.7 18.1 %all_to_all.11 = bf16[4,256,128]{2,1,0:T(8,128)(2,1)S(1)} all-to-all(bf16[4,256,128]{2,1,0:T(8,128)(2,1)S(1)} %pad_maximum_fusion), channel_id=1, replica_groups={{16,8,0,24},{17,9,1,25},{18,10,2,26},{19,11,3,27},{20,12,4,28},{21,13,5..., dimensions={0} | all-to-all | bytes 524288 | tf_op jit(solution)/shard_map/all_to_all | solution.py:327
  86.8 0.7 convert_reduce_fusion
  (4 shorter events, 0.1 us)
Async XLA Ops:
  0.6 48.7 %copy-start = (s32[1,128]{1,0:T(1,128)S(1)}, s32[1,128]{1,0:T(1,128)}, u32[]{:S(2)}) copy-start(s32[1,128]{1,0:T(1,128)} %mask.1) | copy-start | bytes 1540
  28.9 15.4 %collective-permute-start.1 = (bf16[4,272,128]{2,1,0:T(8,128)(2,1)S(1)}, bf16[4,272,128]{2,1,0:T(8,128)(2,1)S(1)}, u32[]{:S(2)}, u32[]{:S(2)}) collective-permute-start(bf16[4,272,128]{2,1,0:T(8,128)(2,1)S(1)} %bitcast.13), channel_id=1, source_target_pairs={{0,96},{32,0},{64,32},{96,64},{1,97},{33,1},{65,33},{97,65},{2,98}... | collective-permute-start | bytes 835592 | tf_op jit(solution)/shard_map/ppermute | solution.py:308
  33.6 14.8 %collective-permute-start = (bf16[4,272,128]{2,1,0:T(8,128)(2,1)S(1)}, bf16[4,272,128]{2,1,0:T(8,128)(2,1)S(1)}, u32[]{:S(2)}, u32[]{:S(2)}) collective-permute-start(bf16[4,272,128]{2,1,0:T(8,128)(2,1)S(1)} %bitcast.14), channel_id=1, source_target_pairs={{0,32},{32,64},{64,96},{96,0},{1,33},{33,65},{65,97},{97,1},{2,34}... | collective-permute-start | bytes 835592 | tf_op jit(solution)/shard_map/ppermute | solution.py:308
  35.5 13.8 %collective-permute-start.2 = (bf16[4,272,128]{2,1,0:T(8,128)(2,1)S(1)}, bf16[4,272,128]{2,1,0:T(8,128)(2,1)S(1)}, u32[]{:S(2)}, u32[]{:S(2)}) collective-permute-start(bf16[4,272,128]{2,1,0:T(8,128)(2,1)S(1)} %bitcast.15), channel_id=1, source_target_pairs={{0,64},{32,96},{64,0},{96,32},{1,65},{33,97},{65,1},{97,33},{2,66}... | collective-permute-start | bytes 835592 | tf_op jit(solution)/shard_map/ppermute | solution.py:308
  39.7 1.0 %copy-start.1 = (bf16[1,128,1024]{2,1,0:T(8,128)(2,1)S(1)}, bf16[1,128,1024]{2,1,0:T(8,128)(2,1)}, u32[]{:S(2)}) copy-start(bf16[1,128,1024]{2,1,0:T(8,128)(2,1)} %param.9) | copy-start | bytes 786436
  40.7 0.9 %copy-start.2 = (bf16[1,128,1024]{2,1,0:T(8,128)(2,1)S(1)}, bf16[1,128,1024]{2,1,0:T(8,128)(2,1)}, u32[]{:S(2)}) copy-start(bf16[1,128,1024]{2,1,0:T(8,128)(2,1)} %param.14) | copy-start | bytes 786436
  41.6 0.8 copy-start.3
  42.4 0.8 copy-start.4

commit v6 on v4

--- a/solution.py
+++ b/solution.py
@@ -9,7 +9,7 @@
 SCALE = HEAD_DIM ** (-0.5)
 LOG2E = 1.4426950408889634
 META = 16
-Z_ORDER = [2, 1, 0, 3]
+Z_ORDER = [2, 3, 0, 1]
 SHIFTS = (0, 1, 3, 2)
 TILE = 512
 NT = (((1,), (1,)), ((), ()))

time: 88.1 us -> 88 us (level)
  the two profiles are of different devices: /device:TPU:48 before, /device:TPU:56 now
where the time goes in v6:
time: 88 us; the launch traced here: 87.5 us
  blocking collectives  58 us (66%)
  starting transfers between devices  10.8 us (12%)
  Pallas kernels  8.24 us (9%)
  local copies, waits for them, and re-layouts  4.09 us (5%)
  waiting for transfers between devices  3.19 us (4%)
  between operations  2.06 us (2%)
  other arithmetic  1.15 us (1%)
    all_gather x1, blocking collectives, body(): column = lax.all_gather(mine, 'gz')  26.1 us
    all_to_all x1, blocking collectives, body(): lax.all_to_all(jnp.stack([partial[i] for i in Z_ORDER]), 'gz', 0, 0, axis...  18.1 us
    all_to_all x1, blocking collectives, body(): terms = lax.all_to_all(prompt_grads, 'gx', 0, 0)  13.8 us
    ppermute x3, starting transfers between devices, shifted(): lax.ppermute(column, 'gx', [(i, (i + shift) % size) for i in range(size)])  10.8 us
    pallas_call x1, Pallas kernels, last_and_backward(): pl.pallas_call(last_kernel, out_shape=(jax.ShapeDtypeStruct((comp_len, wi...  5.33 us
    unnamed x10, local copies, waits for them, and re-layouts  3.41 us
    ppermute x3, waiting for transfers between devices, shifted(): lax.ppermute(column, 'gx', [(i, (i + shift) % size) for i in range(size)])  3.19 us
  transfers between devices with their start and end apart: 3, of which 1 were waited for; matrix products, arithmetic and copies ran while one was open for 0% of the time, Pallas kernels for 3%

profile of v6, /device:TPU:56, one launch (start us, length us, event | category | flops | bytes accessed | tf_op | source)
XLA Modules:
  0.0 87.5 jit_solution(16306842918593398721)
XLA Ops:
  0.6 0.0 copy-start
  2.0 0.1 select_convert_fusion
  2.0 0.8 pad_maximum_fusion.1.mine
  2.8 26.1 %all-gather = bf16[1088,128]{1,0:T(8,128)(2,1)S(1)} all-gather(bf16[272,128]{1,0:T(8,128)(2,1)S(1)} %pad_maximum_fusion.1.mine), channel_id=2, replica_groups=mesh['dp'=4,'gx'=4,'gz'=4,'tensor'=8] {'gz'}, dimensions={0}, use_global_device_ids=true | all-gather | bytes 348160 | tf_op jit(solution)/shard_map/all_gather | solution.py:315
  28.9 4.7 %collective-permute-start.1 = (bf16[4,272,128]{2,1,0:T(8,128)(2,1)S(1)}, bf16[4,272,128]{2,1,0:T(8,128)(2,1)S(1)}, u32[]{:S(2)}, u32[]{:S(2)}) collective-permute-start(bf16[4,272,128]{2,1,0:T(8,128)(2,1)S(1)} %bitcast.13), channel_id=1, source_target_pairs={{0,96},{32,0},{64,32},{96,64},{1,97},{33,1},{65,33},{97,65},{2,98}... | collective-permute-start | bytes 835592 | tf_op jit(solution)/shard_map/ppermute | solution.py:308
  33.6 1.9 %collective-permute-start = (bf16[4,272,128]{2,1,0:T(8,128)(2,1)S(1)}, bf16[4,272,128]{2,1,0:T(8,128)(2,1)S(1)}, u32[]{:S(2)}, u32[]{:S(2)}) collective-permute-start(bf16[4,272,128]{2,1,0:T(8,128)(2,1)S(1)} %bitcast.14), channel_id=1, source_target_pairs={{0,32},{32,64},{64,96},{96,0},{1,33},{33,65},{65,97},{97,1},{2,34}... | collective-permute-start | bytes 835592 | tf_op jit(solution)/shard_map/ppermute | solution.py:308
  35.5 4.2 %collective-permute-start.2 = (bf16[4,272,128]{2,1,0:T(8,128)(2,1)S(1)}, bf16[4,272,128]{2,1,0:T(8,128)(2,1)S(1)}, u32[]{:S(2)}, u32[]{:S(2)}) collective-permute-start(bf16[4,272,128]{2,1,0:T(8,128)(2,1)S(1)} %bitcast.15), channel_id=1, source_target_pairs={{0,64},{32,96},{64,0},{96,32},{1,65},{33,97},{65,1},{97,33},{2,66}... | collective-permute-start | bytes 835592 | tf_op jit(solution)/shard_map/ppermute | solution.py:308
  39.7 0.0 copy-start.1
  39.8 0.9 %copy-done.1 = bf16[1,128,1024]{2,1,0:T(8,128)(2,1)S(1)} copy-done((bf16[1,128,1024]{2,1,0:T(8,128)(2,1)S(1)}, bf16[1,128,1024]{2,1,0:T(8,128)(2,1)}, u32[]{:S(2)}) %copy-start.1) | copy-done | bytes 262168
  40.7 0.0 copy-start.2
  40.7 0.9 %copy-done.2 = bf16[1,128,1024]{2,1,0:T(8,128)(2,1)S(1)} copy-done((bf16[1,128,1024]{2,1,0:T(8,128)(2,1)S(1)}, bf16[1,128,1024]{2,1,0:T(8,128)(2,1)}, u32[]{:S(2)}) %copy-start.2) | copy-done | bytes 262168
  41.6 0.0 copy-start.3
  41.6 0.8 copy-done.3
  42.4 0.0 copy-start.4
  42.4 0.8 copy-done.4
  43.2 1.2 %own_forward.1 = (bf16[1024,128]{1,0:T(8,128)(2,1)S(1)}, bf16[1024,128]{1,0:T(8,128)(2,1)S(1)}, bf16[128,640]{1,0:T(8,128)(2,1)S(1)}, bf16[640,1024]{1,0:T(8,128...) custom-call(bf16[4,272,128]{2,1,0:T(8,128)(2,1)S(1)} %bitcast.16, bf16[128,128]{1,0:T(8,128)(2,1)S(1)} %bitcast.20, ...), custom_call_target="tpu_custom_call" | custom-call | flops 335544320 | tf_op jit(solution)/shard_map/own_forward/pallas_call | solution.py:243
  44.3 0.0 collective-permute-done.1.column.columns_2
  44.4 0.9 near_forward.3
  45.2 3.2 %collective-permute-done.column.columns_1 = bf16[4,272,128]{2,1,0:T(8,128)(2,1)S(1)} collective-permute-done((bf16[4,272,128]{2,1,0:T(8,128)(2,1)S(1)}, bf16[4,272,128]{2,1,0:T(8,128)(2,1)S(1)}, u32[]{:S(2)}, u32[]{:S(2)}) %collective-permute-start) | collective-permute-done | bytes 278560 | tf_op jit(solution)/shard_map/ppermute | solution.py:308
  48.4 0.9 near_forward.2
  49.3 0.0 collective-permute-done.2.columns_3
  49.3 0.0 copy-done
  49.3 5.3 %last_and_backward.1 = (f32[128,1024]{1,0:T(8,128)}, f32[128,128]{1,0:T(8,128)}, f32[128,128]{1,0:T(8,128)}, bf16[4,4,256,128]{3,2,1,0:T(8,128)(2,1)S(1)}) custom-call(s32[1]{0:T(128)} %bitcast.place, bf16[4,272,128]{2,1,0:T(8,128)(2,1)S(1)} %bitcast.17, bf16[4,272,128]{2,1,0:T(8,128)(2,1)S(1)} %collective-permute-done.column.columns_1, ...), custom_call_target="tpu_custom_call" | custom-call | flops 2281701376 | tf_op jit(solution)/shard_map/last_and_backward/pallas_call | solution.py:281
  54.6 13.8 %all_to_all.10 = bf16[4,4,256,128]{3,2,1,0:T(8,128)(2,1)S(1)} all-to-all(bf16[4,4,256,128]{3,2,1,0:T(8,128)(2,1)S(1)} %get-tuple-element.40), channel_id=1, replica_groups=mesh['dp'=4,'gx'=4,'gz'=4,'tensor'=8] {'gx'}, dimensions={0} | all-to-all | bytes 2097152 | tf_op jit(solution)/shard_map/all_to_all | solution.py:325
  68.4 0.2 reduce_sum.21
  68.7 18.1 %all_to_all.11 = bf16[4,256,128]{2,1,0:T(8,128)(2,1)S(1)} all-to-all(bf16[4,256,128]{2,1,0:T(8,128)(2,1)S(1)} %pad_maximum_fusion), channel_id=1, replica_groups={{16,24,0,8},{17,25,1,9},{18,26,2,10},{19,27,3,11},{20,28,4,12},{21,29,5..., dimensions={0} | all-to-all | bytes 524288 | tf_op jit(solution)/shard_map/all_to_all | solution.py:327
  86.8 0.7 fusion.1
  (5 shorter events, 0.1 us)
Async XLA Ops:
  0.6 48.7 %copy-start = (s32[1,128]{1,0:T(1,128)S(1)}, s32[1,128]{1,0:T(1,128)}, u32[]{:S(2)}) copy-start(s32[1,128]{1,0:T(1,128)} %mask.1) | copy-start | bytes 1540
  28.9 15.4 %collective-permute-start.1 = (bf16[4,272,128]{2,1,0:T(8,128)(2,1)S(1)}, bf16[4,272,128]{2,1,0:T(8,128)(2,1)S(1)}, u32[]{:S(2)}, u32[]{:S(2)}) collective-permute-start(bf16[4,272,128]{2,1,0:T(8,128)(2,1)S(1)} %bitcast.13), channel_id=1, source_target_pairs={{0,96},{32,0},{64,32},{96,64},{1,97},{33,1},{65,33},{97,65},{2,98}... | collective-permute-start | bytes 835592 | tf_op jit(solution)/shard_map/ppermute | solution.py:308
  33.6 14.8 %collective-permute-start = (bf16[4,272,128]{2,1,0:T(8,128)(2,1)S(1)}, bf16[4,272,128]{2,1,0:T(8,128)(2,1)S(1)}, u32[]{:S(2)}, u32[]{:S(2)}) collective-permute-start(bf16[4,272,128]{2,1,0:T(8,128)(2,1)S(1)} %bitcast.14), channel_id=1, source_target_pairs={{0,32},{32,64},{64,96},{96,0},{1,33},{33,65},{65,97},{97,1},{2,34}... | collective-permute-start | bytes 835592 | tf_op jit(solution)/shard_map/ppermute | solution.py:308
  35.5 13.8 %collective-permute-start.2 = (bf16[4,272,128]{2,1,0:T(8,128)(2,1)S(1)}, bf16[4,272,128]{2,1,0:T(8,128)(2,1)S(1)}, u32[]{:S(2)}, u32[]{:S(2)}) collective-permute-start(bf16[4,272,128]{2,1,0:T(8,128)(2,1)S(1)} %bitcast.15), channel_id=1, source_target_pairs={{0,64},{32,96},{64,0},{96,32},{1,65},{33,97},{65,1},{97,33},{2,66}... | collective-permute-start | bytes 835592 | tf_op jit(solution)/shard_map/ppermute | solution.py:308
  39.7 1.0 %copy-start.1 = (bf16[1,128,1024]{2,1,0:T(8,128)(2,1)S(1)}, bf16[1,128,1024]{2,1,0:T(8,128)(2,1)}, u32[]{:S(2)}) copy-start(bf16[1,128,1024]{2,1,0:T(8,128)(2,1)} %param.9) | copy-start | bytes 786436
  40.7 0.9 %copy-start.2 = (bf16[1,128,1024]{2,1,0:T(8,128)(2,1)S(1)}, bf16[1,128,1024]{2,1,0:T(8,128)(2,1)}, u32[]{:S(2)}) copy-start(bf16[1,128,1024]{2,1,0:T(8,128)(2,1)} %param.14) | copy-start | bytes 786436
  41.6 0.8 copy-start.3
  42.4 0.8 copy-start.4
